TPU v7x, 256 devices: a whole 4x4x8 slice. The times are simulated.
256 devices in a mesh: seq: 8 (over y, core), tp: 8 (over z), dp: 4 (over x).
Axes of the slice: x: 4, y: 4, z: 8, core: 2. Of those that a mesh axis runs over, the one named last changes fastest.
Arguments:
- queries: bfloat16 [16384, 4096], P(('seq', 'dp'), 'tp'), may hold values from -6 to 6
- keys: bfloat16 [16384, 4096], P(('seq', 'dp'), 'tp'), may hold values from -6 to 6
- values: bfloat16 [16384, 4096], P(('seq', 'dp'), 'tp'), may hold values from -6 to 6
- gain: float32 [4096], P('tp'), may hold values from 0.5 to 2
- out_weight: bfloat16 [4096, 4096], P(('seq', 'dp'), 'tp'), may hold values from -0.09375 to 0.09375
- out_cotangent: bfloat16 [16384, 4096], P(('seq', 'dp'), 'tp'), may hold values from -6 to 6
Outputs:
- query_grad: bfloat16 [16384, 4096], P(('seq', 'dp'), 'tp')
- key_grad: bfloat16 [16384, 4096], P(('seq', 'dp'), 'tp')
- value_grad: bfloat16 [16384, 4096], P(('seq', 'dp'), 'tp')
- gain_grad: float32 [4096], P('tp')
- weight_grad: float32 [4096, 4096], P(('seq', 'dp'), 'tp')
All inputs are finite; a program needn't handle non-finite values.
Results may differ from a plain program's by a relative error of at most 0.023.
Values may be sent and summed in bfloat16 or wider, within the bound.
No kernel may reach another device: no remote copies, remote signals or barrier semaphores. Data moves between devices by JAX's collectives and lax.ppermute only.
A program may use at most 128 MiB of HBM per device.

v0:
```python
import math

import jax
import jax.numpy as jnp
from jax import lax
from jax.experimental import pallas as pl
from jax.experimental.pallas import tpu as pltpu
from jax.sharding import Mesh
from jax.sharding import PartitionSpec as P

HEAD_DIM = 128
HEADS = 4
TOKENS = 512
WIDTH = 512
RING = 8
EPS = 1e-06
SCALE = 1.0 / math.sqrt(16384.0)
BF = jnp.bfloat16
F32 = jnp.float32
PLANE = ("y", "dp")
BLOCKS = ("y", "core", "dp")
VMEM_LIMIT = 24 * 1024 * 1024
STATE = (HEADS * HEAD_DIM, HEAD_DIM)
STATE_GAIN = (HEADS * HEAD_DIM + 16, HEAD_DIM)
SQUARE = (TOKENS, WIDTH)
TOKEN = ((8, HEAD_DIM), jnp.float32)

NN = ((1,), (0,))
NT = ((1,), (1,))
TN = ((0,), (0,))


def dot(a, b, dims):
    return lax.dot_general(a, b, (dims, ((), ())), preferred_element_type=F32)


def span(h):
    return pl.ds(pl.multiple_of(h * HEAD_DIM, HEAD_DIM), HEAD_DIM)


def each(count, step):
    lax.fori_loop(0, count, lambda i, carry: (step(i), carry)[1], 0)


def causal_mask():
    rows = lax.broadcasted_iota(jnp.int32, (TOKENS, TOKENS), 0)
    cols = lax.broadcasted_iota(jnp.int32, (TOKENS, TOKENS), 1)
    return rows >= cols


def call(kernel, out, n_in, flops, any_in=0, scratch=(), any_out=False):
    vmem = pl.BlockSpec(memory_space=pltpu.VMEM)
    anys = pl.BlockSpec(memory_space=pl.ANY)
    return pl.pallas_call(
        kernel,
        out_shape=tuple(jax.ShapeDtypeStruct(s, d) for s, d in out),
        in_specs=[anys] * any_in + [vmem] * n_in,
        out_specs=tuple(anys if any_out else vmem for _ in out),
        scratch_shapes=scratch,
        compiler_params=pltpu.CompilerParams(vmem_limit_bytes=VMEM_LIMIT),
        cost_estimate=pl.CostEstimate(flops=flops, bytes_accessed=4 << 20, transcendentals=0),
    )


def state_kernel(k_ref, v_ref, out_ref, token_ref):
    token_ref[...] = jnp.zeros(TOKEN[0], F32)

    def step(h):
        state = dot(k_ref[:, span(h)], v_ref[:, span(h)], TN).astype(BF)
        out_ref[pl.ds(h * 8, 8)] = state.reshape(8, 16, HEAD_DIM)

    each(HEADS, step)


def scan_kernel(in_ref, out_ref, token_ref):
    token_ref[...] = jnp.zeros(TOKEN[0], F32)
    total = jnp.zeros((16, HEAD_DIM), F32)
    for c in range(32):
        out_ref[c] = total.astype(BF)
        total = total + in_ref[c].astype(F32)


def when(flag):
    return jnp.where(flag, 1.0, 0.0).astype(F32)


def norm_kernel(q_ref, k_ref, v_ref, gain_ref, prior_ref, att_ref, gated_ref):
    mask = causal_mask()

    def step(h):
        cols = span(h)
        scores = dot(q_ref[:, cols], k_ref[:, cols], NT)
        scores = jnp.where(mask, scores, 0.0).astype(BF)
        att = dot(scores, v_ref[:, cols], NN) + dot(q_ref[:, cols], prior_ref[cols], NN)
        att_ref[:, cols] = att
        inverse = lax.rsqrt(jnp.mean(att * att, axis=-1, keepdims=True) + EPS)
        gated = (att * inverse * gain_ref[:, cols]).astype(BF)
        gated_ref[cols, :] = gated.T

    each(HEADS, step)


def is_same():
    return lax.rem(lax.axis_index("tp"), 2) == lax.axis_index("core")


def row_of(k):
    return lax.div(lax.rem(lax.axis_index("tp") + k + RING, RING), 2)


EVENS = (0, 2, -2, 4)
ODDS = (1, -1, 3, -3)


ORDER = (0, 2, -2, 1, -1, 3, -3)


def early_kernel(*refs):
    own, f1, b1, f2, b2, f3, b3, gated_ref, wm_ref, wo_ref = refs[:10]
    sum_ref, part_ref, weight_ref, rows, sems = refs[10:]
    copies = []
    for n, ref in enumerate((own, b2, f2, b1, f1, b3, f3)):
        copies.append(pltpu.make_async_copy(ref, rows.at[n], sems.at[n]))
    for c in copies:
        c.start()
    for c in copies:
        c.wait()
    sum_ref[...] = jnp.zeros(SQUARE, F32)
    same = is_same()

    def offset(n):
        k = jnp.int32(ORDER[-1])
        for i in range(len(ORDER) - 1):
            k = jnp.where(n == i, ORDER[i], k)
        return k

    def fetch(even, k):
        mine = jnp.logical_not(jnp.logical_xor(same, even))
        y = row_of(k)

        @pl.when(mine)
        def _():
            weight_ref[...] = wm_ref[y].reshape(SQUARE)

        @pl.when(jnp.logical_not(mine))
        def _():
            weight_ref[...] = wo_ref[y].reshape(SQUARE)

    def step(n):
        slot = jnp.where(n < 3, n, n + 1)
        part_ref[slot] = dot(gated_ref[...], rows[n], NN).astype(BF)
        fetch(n < 3, offset(n))
        sum_ref[...] += dot(rows[n], weight_ref[...], NN)

    each(7, step)
    fetch(jnp.bool_(True), jnp.int32(4))


def last_kernel(low_ref, high_ref, gated_ref, part_ref, last_ref, other_ref):
    half = TOKENS // 2
    last = dot(gated_ref[:, 0:half], low_ref[...], NN)
    last_ref[...] = (last + dot(gated_ref[:, half:TOKENS], high_ref[...], NN)).astype(BF)
    base = jnp.where(is_same(), 4, 0)

    def step(s):
        other_ref[s] = part_ref[base + s]

    each(3, step)

    @pl.when(is_same())
    def _():
        other_ref[3] = part_ref[7]

    @pl.when(jnp.logical_not(is_same()))
    def _():
        other_ref[3] = last_ref[...]


def grad_kernel(
    low_ref, high_ref, weight_ref, sum_ref, q_ref, att_ref, gain_ref, ga_ref, send_ref, acc
):
    half = TOKENS // 2
    acc[0:half] = sum_ref[0:half] + dot(low_ref[...], weight_ref[...], NN)
    acc[half:TOKENS] = sum_ref[half:TOKENS] + dot(high_ref[...], weight_ref[...], NN)
    grad_rows(acc, q_ref, att_ref, gain_ref, ga_ref, send_ref)


def combine_kernel(
    part_ref, got_ref, last_ref, own_ref, up_ref, down_ref, low_ref, high_ref, rows
):
    place = lax.axis_index("dp")
    same = is_same()
    base = jnp.where(same, 0, 4)

    def step(s):
        late = jnp.logical_and(same, s == 3)

        @pl.when(late)
        def _():
            rows[...] = (last_ref[...].astype(F32) + got_ref[s].astype(F32)).astype(BF)

        @pl.when(jnp.logical_not(late))
        def _():
            rows[...] = (part_ref[base + s].astype(F32) + got_ref[s].astype(F32)).astype(BF)

        blocks = []
        for d in range(4):
            start = pl.multiple_of(lax.rem(place + d, 4) * 128, 128)
            blocks.append(rows[:, pl.ds(start, 128)])
        own_ref[s], up_ref[s], down_ref[s] = blocks[0], blocks[1], blocks[3]
        at = pl.ds(pl.multiple_of(s * 256, 256), 256)
        low_ref[at], high_ref[at] = blocks[2][0:256], blocks[2][256:512]

    each(4, step)


def pack_kernel(after1_ref, after2_ref, own_ref, r1_ref, r2_ref, r3_ref, out_ref, token_ref):
    token_ref[...] = jnp.zeros(TOKEN[0], F32)
    y = lax.axis_index("y")
    for k, ref in enumerate((own_ref, r1_ref, r2_ref, r3_ref)):
        out_ref[lax.rem(y + 4 - k, 4)] = ref[...]


def relay_rows_kernel(after1_ref, after2_ref, low_ref, high_ref, low_out, high_out, sems):
    low = pltpu.make_async_copy(low_ref.at[0:2], low_out, sems.at[0])
    high = pltpu.make_async_copy(high_ref.at[2:4], high_out, sems.at[1])
    low.start()
    high.start()
    low.wait()
    high.wait()


def turn_kernel(
    after_ref, fwd_ref, bwd_ref, own_ref, low_ref, high_ref, far_low_ref, far_high_ref,
    fwd_out, bwd_out, out_ref,
):
    fwd_out[...] = fwd_ref[0 : TOKENS // 2]
    bwd_out[...] = bwd_ref[TOKENS // 2 : TOKENS]
    x = lax.axis_index("dp")
    for k, ref in ((0, own_ref), (3, low_ref), (1, high_ref)):
        for y in range(4):
            out_ref[y, lax.rem(x + k, 4)] = ref[y]
    for y in range(2):
        out_ref[y, lax.rem(x + 2, 4)] = far_low_ref[y]
        out_ref[2 + y, lax.rem(x + 2, 4)] = far_high_ref[y]


def tie(values, deps):
    def kernel(*refs):
        pass

    n = len(values)
    anys = pl.BlockSpec(memory_space=pl.ANY)
    vmem = pl.BlockSpec(memory_space=pltpu.VMEM)
    return pl.pallas_call(
        kernel,
        out_shape=tuple(jax.ShapeDtypeStruct(v.shape, v.dtype) for v in values),
        in_specs=[anys] * n + [vmem] * len(deps),
        out_specs=(anys,) * n,
        input_output_aliases={i: i for i in range(n)},
        cost_estimate=pl.CostEstimate(flops=0, bytes_accessed=0, transcendentals=0),
    )(*values, *deps)


def relay_kernel(after_ref, up_ref, down_ref, low_ref, high_ref, up_out, down_out):
    def step(y):
        rows = pl.ds(pl.multiple_of(y * 256, 256), 256)
        up_out[y, 0:256] = (up_ref[y, 0:256].astype(F32) + low_ref[rows].astype(F32)).astype(BF)
        up_out[y, 256:512] = up_ref[y, 256:512]
        down_out[y, 0:256] = down_ref[y, 0:256]
        low = down_ref[y, 256:512].astype(F32) + high_ref[rows].astype(F32)
        down_out[y, 256:512] = low.astype(BF)

    each(4, step)


def column_kernel(after_ref, own_ref, a_ref, b_ref, own_out, up_out, far_out, down_out, rows):
    same = is_same()

    def step(s):
        k = jnp.where(s == 3, 4, jnp.where(s == 2, -2, s * 2))
        odd = jnp.where(s == 3, -3, jnp.where(s == 2, 3, 1 - 2 * s))
        y = row_of(jnp.where(same, k, odd))
        total = own_ref[s].astype(F32) + a_ref[s].astype(F32) + b_ref[s].astype(F32)
        rows[lax.rem(y + 4 - lax.axis_index("y"), 4)] = total

    each(4, step)
    own_out[...] = rows[0]
    up_out[...] = rows[1].astype(BF)
    far_out[...] = rows[2].astype(BF)
    down_out[...] = rows[3].astype(BF)


def grad_rows(own_ref, q_ref, att_ref, gain_ref, ga_ref, send_ref):
    base = HEADS * HEAD_DIM
    rows = lax.broadcasted_iota(jnp.int32, (16, HEAD_DIM), 0)

    def step(h, sums):
        att = att_ref[:, span(h)]
        inverse = lax.rsqrt(jnp.mean(att * att, axis=-1, keepdims=True) + EPS)
        normed = att * inverse
        grad = own_ref[:, span(h)]
        part = jnp.sum(grad * normed, axis=0, keepdims=True)
        high = part.astype(BF).astype(F32)
        sums = sums + jnp.where(rows == h, high, 0.0) + jnp.where(rows == 4 + h, part - high, 0.0)
        grad = grad * gain_ref[:, span(h)]
        grad = (grad - normed * jnp.mean(grad * normed, axis=-1, keepdims=True)) * inverse
        grad = grad.astype(BF)
        ga_ref[:, span(h)] = grad
        send_ref[span(h)] = dot(q_ref[:, span(h)], grad, TN).astype(BF)
        return sums

    sums = lax.fori_loop(0, HEADS, step, jnp.zeros((16, HEAD_DIM), F32))
    send_ref[base:] = sums.astype(BF)


def resum(parts):
    total = sum(p.astype(F32) for p in parts)
    gain = total[0:4] + total[4:8]
    high = gain.astype(BF).astype(F32)
    return jnp.concatenate([high, gain - high, jnp.zeros((8, HEAD_DIM), F32)], axis=0)


def row_back_kernel(own_ref, r1_ref, r2_ref, r3_ref, total_ref, after_ref):
    x = lax.axis_index("dp")
    base = HEADS * HEAD_DIM
    r1, r2, r3 = (r[0:base].astype(F32) for r in (r1_ref, r2_ref, r3_ref))
    after_ref[...] = r1 * when(x <= 2) + r2 * when(x <= 1) + r3 * when(x <= 0)
    total_ref[0:base] = (own_ref[0:base].astype(F32) + r1 + r2 + r3).astype(BF)
    total_ref[base:] = resum([r[base:] for r in (own_ref, r1_ref, r2_ref, r3_ref)]).astype(BF)


def pair_back_kernel(total_ref, other_ref, out_ref):
    base = HEADS * HEAD_DIM
    out_ref[0:base] = (total_ref[0:base].astype(F32) + other_ref[0:base].astype(F32)).astype(BF)
    out_ref[base:] = resum([total_ref[base:], other_ref[base:]]).astype(BF)


def post_kernel(q_ref, k_ref, v_ref, ga_ref, prior_ref, qg_ref, kp_ref, vp_ref, token_ref):
    token_ref[...] = jnp.zeros(TOKEN[0], F32)
    mask = causal_mask()

    def step(h):
        cols = span(h)
        q, k, v, ga = q_ref[:, cols], k_ref[:, cols], v_ref[:, cols], ga_ref[:, cols]
        scores = jnp.where(mask, dot(q, k, NT), 0.0).astype(BF)
        vp_ref[:, cols] = dot(scores, ga, TN)
        back = jnp.where(mask, dot(ga, v, NT), 0.0).astype(BF)
        qg_ref[:, cols] = (dot(back, k, NN) + dot(ga, prior_ref[cols], NT)).astype(BF)
        kp_ref[:, cols] = dot(back, q, TN)

    each(HEADS, step)


def final_kernel(
    after_last_ref, k_ref, v_ref, kp_ref, vp_ref, after_ref, other_ref, own, u1, u2, u3, kg_ref, vg_ref, gain_ref
):
    base = HEADS * HEAD_DIM
    y = lax.axis_index("y")
    first = when(lax.axis_index("core") == 0)

    def step(h):
        cols = span(h)
        later = after_ref[cols] + other_ref[cols].astype(F32) * first
        later = later + u1[cols].astype(F32) * when(y <= 2) + u2[cols].astype(F32) * when(y <= 1)
        later = (later + u3[cols].astype(F32) * when(y <= 0)).astype(BF)
        kg_ref[:, cols] = (kp_ref[:, cols] + dot(v_ref[:, cols], later, NT)).astype(BF)
        vg_ref[:, cols] = (vp_ref[:, cols] + dot(k_ref[:, cols], later, NN)).astype(BF)

    each(HEADS, step)
    gain = resum([r[base:] for r in (own, u1, u2, u3)])
    gain_ref[...] = (gain[0:4] + gain[4:8]) * SCALE


def sum_kernel(own_ref, r1_ref, r2_ref, r3_ref, out_ref):
    total = own_ref[...]
    for ref in (r1_ref, r2_ref, r3_ref):
        total = total + ref[...].astype(F32)
    out_ref[...] = (total * SCALE).T


def shift(x, axis, size, k, wrap=True):
    pairs = [(i, (i + k) % size) for i in range(size) if wrap or 0 <= i + k < size]
    return lax.ppermute(x, axis, pairs)


def swap_cores(x):
    return lax.ppermute(x, "core", [(0, 1), (1, 0)])


def body(queries, keys, values, gain, out_weight, out_cotangent):
    own = out_cotangent
    fwd, bwd = shift(own, "tp", RING, 1), shift(own, "tp", RING, -1)
    slices = ((32, 16, HEAD_DIM), BF)
    state, state_token = call(state_kernel, [slices, TOKEN], 2, 1 << 27)(keys, values)
    states = lax.all_to_all(state, BLOCKS, 0, 0, tiled=True)
    others = [shift(out_weight, "y", 4, k) for k in (1, 2, 3)]
    column, column_token = call(pack_kernel, [((4, 128, WIDTH), BF), TOKEN], 4, 1 << 20, 2)(
        fwd, bwd, out_weight, *others
    )
    fwd, bwd = tie((fwd, bwd), (state_token, column_token))
    chunks = [own, fwd, bwd]

    fwd, bwd = shift(fwd, "tp", RING, 1), shift(bwd, "tp", RING, -1)
    priors, scan_token = call(scan_kernel, [slices, TOKEN], 1, 1 << 20)(states)
    prior = lax.all_to_all(priors, BLOCKS, 0, 0, tiled=True).reshape(STATE)
    column_low, column_high = shift(column, "dp", 4, 1), shift(column, "dp", 4, -1)
    gain_row = gain.reshape(1, WIDTH)
    att, gated = call(norm_kernel, [(SQUARE, F32), (SQUARE, BF)], 5, 1 << 30)(
        queries, keys, values, gain_row, prior
    )
    relay = ((2, 128, WIDTH), BF)
    relay_low, relay_high = call(
        relay_rows_kernel, [relay, relay], 0, 0, 4, [pltpu.SemaphoreType.DMA((2,))], True
    )(fwd, bwd, column_low, column_high)
    fwd, bwd = tie((fwd, bwd), (scan_token,))
    chunks += [fwd, bwd]

    fwd, bwd = shift(fwd, "tp", RING, 1), shift(bwd, "tp", RING, -1)
    relay_low, relay_high = shift(relay_low, "dp", 4, 1), shift(relay_high, "dp", 4, -1)
    half = ((TOKENS // 2, WIDTH), BF)
    last_low, last_high, weight = call(
        turn_kernel, [half, half, ((4, 4, 128, WIDTH), BF)], 7, 1 << 20, 1
    )(gated, fwd, bwd, column, column_low, column_high, relay_low, relay_high)
    chunks += [fwd, bwd]
    last_low, last_high = shift(last_low, "tp", RING, 1), shift(last_high, "tp", RING, -1)
    weight_other = swap_cores(weight)

    wide = ((8, WIDTH, WIDTH), BF)
    partial_sum, parts, weight_last = call(
        early_kernel,
        [(SQUARE, F32), wide, (SQUARE, BF)],
        3,
        1 << 33,
        7,
        [pltpu.VMEM((7, TOKENS, WIDTH), BF), pltpu.SemaphoreType.DMA((7,))],
    )(*chunks, gated, weight, weight_other)
    last, other = call(last_kernel, [(SQUARE, BF), ((4, WIDTH, WIDTH), BF)], 4, 1 << 29)(
        last_low, last_high, gated, parts
    )
    ga, send = call(
        grad_kernel,
        [(SQUARE, BF), (STATE_GAIN, BF)],
        7,
        1 << 30,
        0,
        [pltpu.VMEM(SQUARE, F32)],
    )(last_low, last_high, weight_last, partial_sum, queries, att, gain_row)
    quarter, eighth = ((4, WIDTH, 128), BF), ((2 * WIDTH, 128), BF)
    part, up, down, low, high = call(
        combine_kernel,
        [quarter, quarter, quarter, eighth, eighth],
        3,
        1 << 20,
        0,
        [pltpu.VMEM(SQUARE, BF)],
    )(parts, swap_cores(other), last)
    total, after = call(row_back_kernel, [(STATE_GAIN, BF), (STATE, F32)], 4, 1 << 22)(
        send, *[shift(send, "dp", 4, -k) for k in (1, 2, 3)]
    )
    up, down = call(relay_kernel, [quarter, quarter], 4, 1 << 20, 1)(
        total, up, down, shift(low, "dp", 4, 1), shift(high, "dp", 4, -1)
    )
    query_grad, key_part, value_part, token = call(
        post_kernel, [(SQUARE, BF), (SQUARE, F32), (SQUARE, F32), TOKEN], 5, 1 << 31
    )(queries, keys, values, ga, prior)
    block = (WIDTH, 128)
    part, up, away, down = call(
        column_kernel,
        [(block, F32), (block, BF), (block, BF), (block, BF)],
        4,
        1 << 20,
        0,
        [pltpu.VMEM((4, WIDTH, 128), F32)],
    )(token, part, shift(up, "dp", 4, 1), shift(down, "dp", 4, -1))
    (weight_grad,) = call(sum_kernel, [((128, WIDTH), F32)], 4, 1 << 20)(
        part, shift(up, "y", 4, 1), shift(away, "y", 4, 2), shift(down, "y", 4, -1)
    )
    other = swap_cores(total)
    (both,) = call(pair_back_kernel, [(STATE_GAIN, BF)], 2, 1 << 22)(total, other)
    upper = [shift(both, "y", 4, -k) for k in (1, 2, 3)]
    key_grad, value_grad, gain_sum = call(
        final_kernel, [(SQUARE, BF), (SQUARE, BF), ((HEADS, HEAD_DIM), F32)], 10, 1 << 28, 1
    )(down, keys, values, key_part, value_part, after, other, both, *upper)
    gain_grad = gain_sum.reshape(WIDTH)
    return query_grad, key_grad, value_grad, gain_grad, weight_grad


def solution(mesh):
    grid = Mesh(mesh.devices.reshape(4, 2, RING, 4), ("y", "core", "tp", "dp"))
    rows = P(("y", "core", "dp"), "tp")
    return jax.shard_map(
        body,
        mesh=grid,
        in_specs=(rows, rows, rows, P("tp"), rows, rows),
        out_specs=(rows, rows, rows, P("tp"), rows),
        check_vma=False,
    )
```

profile of v0, /device:TPU:6, one launch (start us, length us, event | category | flops | bytes accessed | tf_op | source)
XLA Modules:
  0.0 127.6 jit_solution(16568534243913844578)
XLA Ops:
  0.6 2.0 %collective-permute-start = (bf16[512,512]{1,0:T(8,128)(2,1)}, bf16[512,512]{1,0:T(8,128)(2,1)S(1)}, u32[]{:S(2)}, u32[]{:S(2)}) collective-permute-start(bf16[512,512]{1,0:T(8,128)(2,1)} %refs_0_.1), channel_id=1, source_target_pairs={{0,4},{4,8},{8,12},{12,16},{16,20},{20,24},{24,28},{28,0},{1,5},{5... | collective-permute-start | bytes 1572872 | tf_op jit(solution)/shard_map/ppermute | solution.py:384
  2.6 4.0 %collective-permute-start.1 = (bf16[512,512]{1,0:T(8,128)(2,1)}, bf16[512,512]{1,0:T(8,128)(2,1)S(1)}, u32[]{:S(2)}, u32[]{:S(2)}) collective-permute-start(bf16[512,512]{1,0:T(8,128)(2,1)} %refs_0_.1), channel_id=1, source_target_pairs={{0,28},{4,0},{8,4},{12,8},{16,12},{20,16},{24,20},{28,24},{1,29},{... | collective-permute-start | bytes 1572872 | tf_op jit(solution)/shard_map/ppermute | solution.py:384
  6.7 3.2 %collective-permute-start.3 = (bf16[128,512]{1,0:T(8,128)(2,1)}, bf16[128,512]{1,0:T(8,128)(2,1)S(1)}, u32[]{:S(2)}, u32[]{:S(2)}) collective-permute-start(bf16[128,512]{1,0:T(8,128)(2,1)} %own_ref.1), channel_id=1, source_target_pairs={{0,128},{64,192},{128,0},{192,64},{1,129},{65,193},{129,1},{193,65... | collective-permute-start | bytes 393224 | tf_op jit(solution)/shard_map/ppermute | solution.py:384
  10.5 2.6 %collective-permute-start.4 = (bf16[128,512]{1,0:T(8,128)(2,1)}, bf16[128,512]{1,0:T(8,128)(2,1)S(1)}, u32[]{:S(2)}, u32[]{:S(2)}) collective-permute-start(bf16[128,512]{1,0:T(8,128)(2,1)} %own_ref.1), channel_id=1, source_target_pairs={{0,192},{64,0},{128,64},{192,128},{1,193},{65,1},{129,65},{193,129... | collective-permute-start | bytes 393224 | tf_op jit(solution)/shard_map/ppermute | solution.py:384
  16.7 2.0 %collective-permute-done.after1_ref.refs_0_ = bf16[512,512]{1,0:T(8,128)(2,1)S(1)} collective-permute-done((bf16[512,512]{1,0:T(8,128)(2,1)}, bf16[512,512]{1,0:T(8,128)(2,1)S(1)}, u32[]{:S(2)}, u32[]{:S(2)}) %collective-permute-start) | collective-permute-done | bytes 524320 | tf_op jit(solution)/shard_map/ppermute | solution.py:384
  22.0 3.2 %collective-permute-start.6 = (bf16[512,512]{1,0:T(8,128)(2,1)}, bf16[512,512]{1,0:T(8,128)(2,1)S(1)}, u32[]{:S(2)}, u32[]{:S(2)}) collective-permute-start(bf16[512,512]{1,0:T(8,128)(2,1)} %get-tuple-element.55.refs_2_), channel_id=1, source_target_pairs={{0,28},{4,0},{8,4},{12,8},{16,12},{20,16},{24,20},{28,24},{1,29},{... | collective-permute-start | bytes 1572872 | tf_op jit(solution)/shard_map/ppermute | solution.py:384
  26.1 2.4 %collective-permute-start.9 = (bf16[4,128,512]{2,1,0:T(8,128)(2,1)}, bf16[4,128,512]{2,1,0:T(8,128)(2,1)S(1)}, u32[]{:S(2)}, u32[]{:S(2)}) collective-permute-start(bf16[4,128,512]{2,1,0:T(8,128)(2,1)} %get-tuple-element.59.own_ref), channel_id=1, source_target_pairs={{0,1},{1,2},{2,3},{3,0},{4,5},{5,6},{6,7},{7,4},{8,9},{9,10},{10,1... | collective-permute-start | bytes 1572872 | tf_op jit(solution)/shard_map/ppermute | solution.py:384
  28.5 14.5 %all_to_all.10.in_ref = bf16[32,16,128]{2,1,0:T(8,128)(2,1)S(1)} all-to-all(bf16[32,16,128]{2,1,0:T(8,128)(2,1)S(1)} %get-tuple-element.49), channel_id=1, replica_groups=mesh['y'=4,'core'=2,'tp'=8,'dp'=4] {'y','core','dp'}, dimensions={0} | all-to-all | bytes 262144 | tf_op jit(solution)/shard_map/all_to_all | solution.py:396
  45.4 3.2 %collective-permute-start.8 = (bf16[512,512]{1,0:T(8,128)(2,1)}, bf16[512,512]{1,0:T(8,128)(2,1)S(1)}, u32[]{:S(2)}, u32[]{:S(2)}) collective-permute-start(bf16[512,512]{1,0:T(8,128)(2,1)} %get-tuple-element.58.refs_4_), channel_id=1, source_target_pairs={{0,28},{4,0},{8,4},{12,8},{16,12},{20,16},{24,20},{28,24},{1,29},{... | collective-permute-start | bytes 1572872 | tf_op jit(solution)/shard_map/ppermute | solution.py:384
  48.6 3.2 %collective-permute-start.11 = (bf16[2,128,512]{2,1,0:T(8,128)(2,1)}, bf16[2,128,512]{2,1,0:T(8,128)(2,1)S(1)}, u32[]{:S(2)}, u32[]{:S(2)}) collective-permute-start(bf16[2,128,512]{2,1,0:T(8,128)(2,1)} %copy-done.19), channel_id=1, source_target_pairs={{0,1},{1,2},{2,3},{3,0},{4,5},{5,6},{6,7},{7,4},{8,9},{9,10},{10,1... | collective-permute-start | bytes 786440 | tf_op jit(solution)/shard_map/ppermute | solution.py:384
  51.8 12.2 %all_to_all.11 = bf16[32,16,128]{2,1,0:T(8,128)(2,1)S(1)} all-to-all(bf16[32,16,128]{2,1,0:T(8,128)(2,1)S(1)} %get-tuple-element.50), channel_id=1, replica_groups=mesh['y'=4,'core'=2,'tp'=8,'dp'=4] {'y','core','dp'}, dimensions={0} | all-to-all | bytes 262144 | tf_op jit(solution)/shard_map/all_to_all | solution.py:406
  65.1 2.5 %shard_map.103 = (f32[512,512]{1,0:T(8,128)S(1)}, bf16[512,512]{1,0:T(8,128)(2,1)S(1)}) custom-call(bf16[512,512]{1,0:T(8,128)(2,1)S(1)} %copy-done.17, bf16[512,512]{1,0:T(8,128)(2,1)S(1)} %copy-done.1, bf16[512,512]{1,0:T(8,128)(2,1)S(1)} %copy-done.3, f32[1,512]{1,0:T(1,128)S(1)} %bitcast.5, bf16[512,128]{1,0:T(8,128)(2,1)S(1)} %bitcast.3), custom_call_target="tpu_custom_call" | custom-call | flops 1073741824 | bytes 4194304 | tf_op jit(solution)/shard_map/pallas_call | solution.py:409
  69.4 3.2 %collective-permute-start.14 = (bf16[256,512]{1,0:T(8,128)(2,1)S(1)}, bf16[256,512]{1,0:T(8,128)(2,1)S(1)}, u32[]{:S(2)}, u32[]{:S(2)}) collective-permute-start(bf16[256,512]{1,0:T(8,128)(2,1)S(1)} %get-tuple-element.63), channel_id=1, source_target_pairs={{0,28},{4,0},{8,4},{12,8},{16,12},{20,16},{24,20},{28,24},{1,29},{... | collective-permute-start | bytes 786440 | tf_op jit(solution)/shard_map/ppermute | solution.py:384
  73.5 6.8 %shard_map.109 = (f32[512,512]{1,0:T(8,128)S(1)}, bf16[8,512,512]{2,1,0:T(8,128)(2,1)S(1)}, bf16[512,512]{1,0:T(8,128)(2,1)S(1)}) custom-call(bf16[512,512]{1,0:T(8,128)(2,1)S(1)} %copy-done.16, bf16[512,512]{1,0:T(8,128)(2,1)S(1)} %copy-done.5, bf16[512,512]{1,0:T(8,128)(2,1)S(1)} %copy-done.7, bf16[512,512]{1,0:T(8,128)(2,1)S(1)} %copy-done.9, ...), custom_call_target="tpu_custom_call" | custom-call | flops 8589934592 | bytes 4194304 | tf_op jit(solution)/shard_map/pallas_call | solution.py:430
  81.1 4.0 %collective-permute-done.16.got_ref = bf16[4,512,512]{2,1,0:T(8,128)(2,1)S(1)} collective-permute-done((bf16[4,512,512]{2,1,0:T(8,128)(2,1)S(1)}, bf16[4,512,512]{2,1,0:T(8,128)(2,1)S(1)}, u32[]{:S(2)}, u32[]{:S(2)}) %collective-permute-start.16) | collective-permute-done | bytes 2097184 | tf_op jit(solution)/shard_map/ppermute | solution.py:388
  88.2 2.1 %shard_map.110 = (bf16[512,512]{1,0:T(8,128)(2,1)S(1)}, bf16[528,128]{1,0:T(8,128)(2,1)S(1)}) custom-call(bf16[256,512]{1,0:T(8,128)(2,1)S(1)} %collective-permute-done.13.low_ref, bf16[256,512]{1,0:T(8,128)(2,1)S(1)} %collective-permute-done.14.high_ref, bf16[512,512]{1,0:T(8,128)(2,1)S(1)} %get-tuple-element.65.weight_ref, ...), custom_call_target="tpu_custom_call" | custom-call | flops 1073741824 | bytes 4194304 | tf_op jit(solution)/shard_map/pallas_call | solution.py:441
  90.3 3.0 %collective-permute-start.19 = (bf16[528,128]{1,0:T(8,128)(2,1)S(1)}, bf16[528,128]{1,0:T(8,128)(2,1)S(1)}, u32[]{:S(2)}, u32[]{:S(2)}) collective-permute-start(bf16[528,128]{1,0:T(8,128)(2,1)S(1)} %get-tuple-element.75.own_ref), channel_id=1, source_target_pairs={{0,1},{1,2},{2,3},{3,0},{4,5},{5,6},{6,7},{7,4},{8,9},{9,10},{10,1... | collective-permute-start | bytes 405512 | tf_op jit(solution)/shard_map/ppermute | solution.py:384
  94.2 5.4 %collective-permute-done.19.r3_ref = bf16[528,128]{1,0:T(8,128)(2,1)S(1)} collective-permute-done((bf16[528,128]{1,0:T(8,128)(2,1)S(1)}, bf16[528,128]{1,0:T(8,128)(2,1)S(1)}, u32[]{:S(2)}, u32[]{:S(2)}) %collective-permute-start.19) | collective-permute-done | bytes 135200 | tf_op jit(solution)/shard_map/ppermute | solution.py:384
  101.2 1.8 %collective-permute-done.17.r1_ref = bf16[528,128]{1,0:T(8,128)(2,1)S(1)} collective-permute-done((bf16[528,128]{1,0:T(8,128)(2,1)S(1)}, bf16[528,128]{1,0:T(8,128)(2,1)S(1)}, u32[]{:S(2)}, u32[]{:S(2)}) %collective-permute-start.17) | collective-permute-done | bytes 135200 | tf_op jit(solution)/shard_map/ppermute | solution.py:384
  107.5 2.0 %collective-permute-start.26 = (bf16[528,128]{1,0:T(8,128)(2,1)S(1)}, bf16[528,128]{1,0:T(8,128)(2,1)S(1)}, u32[]{:S(2)}, u32[]{:S(2)}) collective-permute-start(bf16[528,128]{1,0:T(8,128)(2,1)S(1)} %shard_map.117.own), channel_id=1, source_target_pairs={{0,128},{64,192},{128,0},{192,64},{1,129},{65,193},{129,1},{193,65... | collective-permute-start | bytes 405512 | tf_op jit(solution)/shard_map/ppermute | solution.py:384
  110.8 4.4 %shard_map.111 = (bf16[512,512]{1,0:T(8,128)(2,1)}, f32[512,512]{1,0:T(8,128)S(1)}, f32[512,512]{1,0:T(8,128)S(1)}, f32[8,128]{1,0:T(8,128)S(1)}) custom-call(bf16[512,512]{1,0:T(8,128)(2,1)S(1)} %copy-done.18, bf16[512,512]{1,0:T(8,128)(2,1)S(1)} %copy-done.1, bf16[512,512]{1,0:T(8,128)(2,1)S(1)} %copy-done.3, ...), custom_call_target="tpu_custom_call" | custom-call | flops 2147483648 | bytes 4194304 | tf_op jit(solution)/shard_map/pallas_call | solution.py:464
  118.9 2.0 %collective-permute-start.29 = (bf16[512,128]{1,0:T(8,128)(2,1)S(1)}, bf16[512,128]{1,0:T(8,128)(2,1)S(1)}, u32[]{:S(2)}, u32[]{:S(2)}) collective-permute-start(bf16[512,128]{1,0:T(8,128)(2,1)S(1)} %get-tuple-element.92), channel_id=1, source_target_pairs={{0,128},{64,192},{128,0},{192,64},{1,129},{65,193},{129,1},{193,65... | collective-permute-start | bytes 393224 | tf_op jit(solution)/shard_map/ppermute | solution.py:384
  122.3 1.9 %shard_map.118 = (bf16[512,512]{1,0:T(8,128)(2,1)}, bf16[512,512]{1,0:T(8,128)(2,1)}, f32[4,128]{1,0:T(4,128)}) custom-call(bf16[512,128]{1,0:T(8,128)(2,1)S(1)} %get-tuple-element.83.after_last_ref, bf16[512,512]{1,0:T(8,128)(2,1)S(1)} %copy-done.1, bf16[512,512]{1,0:T(8,128)(2,1)S(1)} %copy-done.3, f32[512,512]{1,0:T(8,128)S(1)} %get-tuple-element.84.kp_ref, ...), custom_call_target="tpu_custom_call" | custom-call | flops 268435456 | bytes 4194304 | tf_op jit(solution)/shard_map/pallas_call | solution.py:482
  124.2 1.9 %collective-permute-done.28.r1_ref = bf16[512,128]{1,0:T(8,128)(2,1)S(1)} collective-permute-done((bf16[512,128]{1,0:T(8,128)(2,1)S(1)}, bf16[512,128]{1,0:T(8,128)(2,1)S(1)}, u32[]{:S(2)}, u32[]{:S(2)}) %collective-permute-start.28) | collective-permute-done | bytes 131104 | tf_op jit(solution)/shard_map/ppermute | solution.py:384
  (101 shorter events, 33.3 us)
Async XLA Ops:
  0.6 18.1 %collective-permute-start = (bf16[512,512]{1,0:T(8,128)(2,1)}, bf16[512,512]{1,0:T(8,128)(2,1)S(1)}, u32[]{:S(2)}, u32[]{:S(2)}) collective-permute-start(bf16[512,512]{1,0:T(8,128)(2,1)} %refs_0_.1), channel_id=1, source_target_pairs={{0,4},{4,8},{8,12},{12,16},{16,20},{20,24},{24,28},{28,0},{1,5},{5... | collective-permute-start | bytes 1572872 | tf_op jit(solution)/shard_map/ppermute | solution.py:384
  2.6 16.1 %collective-permute-start.1 = (bf16[512,512]{1,0:T(8,128)(2,1)}, bf16[512,512]{1,0:T(8,128)(2,1)S(1)}, u32[]{:S(2)}, u32[]{:S(2)}) collective-permute-start(bf16[512,512]{1,0:T(8,128)(2,1)} %refs_0_.1), channel_id=1, source_target_pairs={{0,28},{4,0},{8,4},{12,8},{16,12},{20,16},{24,20},{28,24},{1,29},{... | collective-permute-start | bytes 1572872 | tf_op jit(solution)/shard_map/ppermute | solution.py:384
  6.7 10.0 %collective-permute-start.3 = (bf16[128,512]{1,0:T(8,128)(2,1)}, bf16[128,512]{1,0:T(8,128)(2,1)S(1)}, u32[]{:S(2)}, u32[]{:S(2)}) collective-permute-start(bf16[128,512]{1,0:T(8,128)(2,1)} %own_ref.1), channel_id=1, source_target_pairs={{0,128},{64,192},{128,0},{192,64},{1,129},{65,193},{129,1},{193,65... | collective-permute-start | bytes 393224 | tf_op jit(solution)/shard_map/ppermute | solution.py:384
  21.9 21.7 %collective-permute-start.5 = (bf16[512,512]{1,0:T(8,128)(2,1)}, bf16[512,512]{1,0:T(8,128)(2,1)S(1)}, u32[]{:S(2)}, u32[]{:S(2)}) collective-permute-start(bf16[512,512]{1,0:T(8,128)(2,1)} %get-tuple-element.54.refs_1_), channel_id=1, source_target_pairs={{0,4},{4,8},{8,12},{12,16},{16,20},{20,24},{24,28},{28,0},{1,5},{5... | collective-permute-start | bytes 1572872 | tf_op jit(solution)/shard_map/ppermute | solution.py:384
  22.0 21.6 %collective-permute-start.6 = (bf16[512,512]{1,0:T(8,128)(2,1)}, bf16[512,512]{1,0:T(8,128)(2,1)S(1)}, u32[]{:S(2)}, u32[]{:S(2)}) collective-permute-start(bf16[512,512]{1,0:T(8,128)(2,1)} %get-tuple-element.55.refs_2_), channel_id=1, source_target_pairs={{0,28},{4,0},{8,4},{12,8},{16,12},{20,16},{24,20},{28,24},{1,29},{... | collective-permute-start | bytes 1572872 | tf_op jit(solution)/shard_map/ppermute | solution.py:384
  25.2 18.4 %collective-permute-start.10 = (bf16[4,128,512]{2,1,0:T(8,128)(2,1)}, bf16[4,128,512]{2,1,0:T(8,128)(2,1)S(1)}, u32[]{:S(2)}, u32[]{:S(2)}) collective-permute-start(bf16[4,128,512]{2,1,0:T(8,128)(2,1)} %get-tuple-element.59.own_ref), channel_id=1, source_target_pairs={{0,3},{1,0},{2,1},{3,2},{4,7},{5,4},{6,5},{7,6},{8,11},{9,8},{10,9... | collective-permute-start | bytes 1572872 | tf_op jit(solution)/shard_map/ppermute | solution.py:384
  26.1 17.6 %collective-permute-start.9 = (bf16[4,128,512]{2,1,0:T(8,128)(2,1)}, bf16[4,128,512]{2,1,0:T(8,128)(2,1)S(1)}, u32[]{:S(2)}, u32[]{:S(2)}) collective-permute-start(bf16[4,128,512]{2,1,0:T(8,128)(2,1)} %get-tuple-element.59.own_ref), channel_id=1, source_target_pairs={{0,1},{1,2},{2,3},{3,0},{4,5},{5,6},{6,7},{7,4},{8,9},{9,10},{10,1... | collective-permute-start | bytes 1572872 | tf_op jit(solution)/shard_map/ppermute | solution.py:384
  45.4 22.3 %collective-permute-start.7 = (bf16[512,512]{1,0:T(8,128)(2,1)}, bf16[512,512]{1,0:T(8,128)(2,1)S(1)}, u32[]{:S(2)}, u32[]{:S(2)}) collective-permute-start(bf16[512,512]{1,0:T(8,128)(2,1)} %get-tuple-element.57.refs_3_), channel_id=1, source_target_pairs={{0,4},{4,8},{8,12},{12,16},{16,20},{20,24},{24,28},{28,0},{1,5},{5... | collective-permute-start | bytes 1572872 | tf_op jit(solution)/shard_map/ppermute | solution.py:384
  45.4 22.3 %collective-permute-start.8 = (bf16[512,512]{1,0:T(8,128)(2,1)}, bf16[512,512]{1,0:T(8,128)(2,1)S(1)}, u32[]{:S(2)}, u32[]{:S(2)}) collective-permute-start(bf16[512,512]{1,0:T(8,128)(2,1)} %get-tuple-element.58.refs_4_), channel_id=1, source_target_pairs={{0,28},{4,0},{8,4},{12,8},{16,12},{20,16},{24,20},{28,24},{1,29},{... | collective-permute-start | bytes 1572872 | tf_op jit(solution)/shard_map/ppermute | solution.py:384
  48.6 19.0 %collective-permute-start.11 = (bf16[2,128,512]{2,1,0:T(8,128)(2,1)}, bf16[2,128,512]{2,1,0:T(8,128)(2,1)S(1)}, u32[]{:S(2)}, u32[]{:S(2)}) collective-permute-start(bf16[2,128,512]{2,1,0:T(8,128)(2,1)} %copy-done.19), channel_id=1, source_target_pairs={{0,1},{1,2},{2,3},{3,0},{4,5},{5,6},{6,7},{7,4},{8,9},{9,10},{10,1... | collective-permute-start | bytes 786440 | tf_op jit(solution)/shard_map/ppermute | solution.py:384
  51.8 15.8 %collective-permute-start.12 = (bf16[2,128,512]{2,1,0:T(8,128)(2,1)S(1)}, bf16[2,128,512]{2,1,0:T(8,128)(2,1)S(1)}, u32[]{:S(2)}, u32[]{:S(2)}) collective-permute-start(bf16[2,128,512]{2,1,0:T(8,128)(2,1)S(1)} %get-tuple-element.61), channel_id=1, source_target_pairs={{0,3},{1,0},{2,1},{3,2},{4,7},{5,4},{6,5},{7,6},{8,11},{9,8},{10,9... | collective-permute-start | bytes 786440 | tf_op jit(solution)/shard_map/ppermute | solution.py:384
  69.3 11.0 %collective-permute-start.13 = (bf16[256,512]{1,0:T(8,128)(2,1)S(1)}, bf16[256,512]{1,0:T(8,128)(2,1)S(1)}, u32[]{:S(2)}, u32[]{:S(2)}) collective-permute-start(bf16[256,512]{1,0:T(8,128)(2,1)S(1)} %get-tuple-element.62), channel_id=1, source_target_pairs={{0,4},{4,8},{8,12},{12,16},{16,20},{20,24},{24,28},{28,0},{1,5},{5... | collective-permute-start | bytes 786440 | tf_op jit(solution)/shard_map/ppermute | solution.py:384
  69.4 10.9 %collective-permute-start.14 = (bf16[256,512]{1,0:T(8,128)(2,1)S(1)}, bf16[256,512]{1,0:T(8,128)(2,1)S(1)}, u32[]{:S(2)}, u32[]{:S(2)}) collective-permute-start(bf16[256,512]{1,0:T(8,128)(2,1)S(1)} %get-tuple-element.63), channel_id=1, source_target_pairs={{0,28},{4,0},{8,4},{12,8},{16,12},{20,16},{24,20},{28,24},{1,29},{... | collective-permute-start | bytes 786440 | tf_op jit(solution)/shard_map/ppermute | solution.py:384
  86.1 17.1 %collective-permute-start.20 = (bf16[1024,128]{1,0:T(8,128)(2,1)S(1)}, bf16[1024,128]{1,0:T(8,128)(2,1)S(1)}, u32[]{:S(2)}, u32[]{:S(2)}) collective-permute-start(bf16[1024,128]{1,0:T(8,128)(2,1)S(1)} %get-tuple-element.79), channel_id=1, source_target_pairs={{0,1},{1,2},{2,3},{3,0},{4,5},{5,6},{6,7},{7,4},{8,9},{9,10},{10,1... | collective-permute-start | bytes 786440 | tf_op jit(solution)/shard_map/ppermute | solution.py:384
  87.8 15.3 %collective-permute-start.21 = (bf16[1024,128]{1,0:T(8,128)(2,1)S(1)}, bf16[1024,128]{1,0:T(8,128)(2,1)S(1)}, u32[]{:S(2)}, u32[]{:S(2)}) collective-permute-start(bf16[1024,128]{1,0:T(8,128)(2,1)S(1)} %get-tuple-element.80), channel_id=1, source_target_pairs={{0,3},{1,0},{2,1},{3,2},{4,7},{5,4},{6,5},{7,6},{8,11},{9,8},{10,9... | collective-permute-start | bytes 786440 | tf_op jit(solution)/shard_map/ppermute | solution.py:384
  90.3 9.3 %collective-permute-start.19 = (bf16[528,128]{1,0:T(8,128)(2,1)S(1)}, bf16[528,128]{1,0:T(8,128)(2,1)S(1)}, u32[]{:S(2)}, u32[]{:S(2)}) collective-permute-start(bf16[528,128]{1,0:T(8,128)(2,1)S(1)} %get-tuple-element.75.own_ref), channel_id=1, source_target_pairs={{0,1},{1,2},{2,3},{3,0},{4,5},{5,6},{6,7},{7,4},{8,9},{9,10},{10,1... | collective-permute-start | bytes 405512 | tf_op jit(solution)/shard_map/ppermute | solution.py:384
  93.3 7.9 %collective-permute-start.18 = (bf16[528,128]{1,0:T(8,128)(2,1)S(1)}, bf16[528,128]{1,0:T(8,128)(2,1)S(1)}, u32[]{:S(2)}, u32[]{:S(2)}) collective-permute-start(bf16[528,128]{1,0:T(8,128)(2,1)S(1)} %get-tuple-element.75.own_ref), channel_id=1, source_target_pairs={{0,2},{1,3},{2,0},{3,1},{4,6},{5,7},{6,4},{7,5},{8,10},{9,11},{10,... | collective-permute-start | bytes 405512 | tf_op jit(solution)/shard_map/ppermute | solution.py:384
  93.3 9.7 %collective-permute-start.17 = (bf16[528,128]{1,0:T(8,128)(2,1)S(1)}, bf16[528,128]{1,0:T(8,128)(2,1)S(1)}, u32[]{:S(2)}, u32[]{:S(2)}) collective-permute-start(bf16[528,128]{1,0:T(8,128)(2,1)S(1)} %get-tuple-element.75.own_ref), channel_id=1, source_target_pairs={{0,3},{1,0},{2,1},{3,2},{4,7},{5,4},{6,5},{7,6},{8,11},{9,8},{10,9... | collective-permute-start | bytes 405512 | tf_op jit(solution)/shard_map/ppermute | solution.py:384
  103.3 13.4 %collective-permute-start.22 = (bf16[4,512,128]{2,1,0:T(8,128)(2,1)S(1)}, bf16[4,512,128]{2,1,0:T(8,128)(2,1)S(1)}, u32[]{:S(2)}, u32[]{:S(2)}) collective-permute-start(bf16[4,512,128]{2,1,0:T(8,128)(2,1)S(1)} %get-tuple-element.81), channel_id=1, source_target_pairs={{0,1},{1,2},{2,3},{3,0},{4,5},{5,6},{6,7},{7,4},{8,9},{9,10},{10,1... | collective-permute-start | bytes 1572872 | tf_op jit(solution)/shard_map/ppermute | solution.py:384
  103.7 14.3 %collective-permute-start.23 = (bf16[4,512,128]{2,1,0:T(8,128)(2,1)S(1)}, bf16[4,512,128]{2,1,0:T(8,128)(2,1)S(1)}, u32[]{:S(2)}, u32[]{:S(2)}) collective-permute-start(bf16[4,512,128]{2,1,0:T(8,128)(2,1)S(1)} %get-tuple-element.82), channel_id=1, source_target_pairs={{0,3},{1,0},{2,1},{3,2},{4,7},{5,4},{6,5},{7,6},{8,11},{9,8},{10,9... | collective-permute-start | bytes 1572872 | tf_op jit(solution)/shard_map/ppermute | solution.py:384
  106.8 14.1 %collective-permute-start.27 = (bf16[528,128]{1,0:T(8,128)(2,1)S(1)}, bf16[528,128]{1,0:T(8,128)(2,1)S(1)}, u32[]{:S(2)}, u32[]{:S(2)}) collective-permute-start(bf16[528,128]{1,0:T(8,128)(2,1)S(1)} %shard_map.117.own), channel_id=1, source_target_pairs={{0,64},{64,128},{128,192},{192,0},{1,65},{65,129},{129,193},{193,1... | collective-permute-start | bytes 405512 | tf_op jit(solution)/shard_map/ppermute | solution.py:384
  107.5 14.8 %collective-permute-start.26 = (bf16[528,128]{1,0:T(8,128)(2,1)S(1)}, bf16[528,128]{1,0:T(8,128)(2,1)S(1)}, u32[]{:S(2)}, u32[]{:S(2)}) collective-permute-start(bf16[528,128]{1,0:T(8,128)(2,1)S(1)} %shard_map.117.own), channel_id=1, source_target_pairs={{0,128},{64,192},{128,0},{192,64},{1,129},{65,193},{129,1},{193,65... | collective-permute-start | bytes 405512 | tf_op jit(solution)/shard_map/ppermute | solution.py:384
  109.5 12.8 %collective-permute-start.25 = (bf16[528,128]{1,0:T(8,128)(2,1)S(1)}, bf16[528,128]{1,0:T(8,128)(2,1)S(1)}, u32[]{:S(2)}, u32[]{:S(2)}) collective-permute-start(bf16[528,128]{1,0:T(8,128)(2,1)S(1)} %shard_map.117.own), channel_id=1, source_target_pairs={{0,192},{64,0},{128,64},{192,128},{1,193},{65,1},{129,65},{193,129... | collective-permute-start | bytes 405512 | tf_op jit(solution)/shard_map/ppermute | solution.py:384
  118.3 7.8 %collective-permute-start.28 = (bf16[512,128]{1,0:T(8,128)(2,1)S(1)}, bf16[512,128]{1,0:T(8,128)(2,1)S(1)}, u32[]{:S(2)}, u32[]{:S(2)}) collective-permute-start(bf16[512,128]{1,0:T(8,128)(2,1)S(1)} %get-tuple-element.91), channel_id=1, source_target_pairs={{0,64},{64,128},{128,192},{192,0},{1,65},{65,129},{129,193},{193,1... | collective-permute-start | bytes 393224 | tf_op jit(solution)/shard_map/ppermute | solution.py:384
  (28 other events, 207.6 us)
where the time goes:
time: 128 us
  starting transfers between devices  45.4 us (35%)
  blocking collectives  26.7 us (21%)
  Pallas kernels  25.3 us (20%)
  waiting for transfers between devices  22.3 us (17%)
  local copies, waits for them, and re-layouts  6.95 us (5%)
    ppermute x28, starting transfers between devices, shift(): return lax.ppermute(x, axis, pairs)  44.9 us
    ppermute x28, waiting for transfers between devices, shift(): return lax.ppermute(x, axis, pairs)  16.1 us
    all_to_all x1, blocking collectives, body(): states = lax.all_to_all(state, BLOCKS, 0, 0, tiled=True)  14.5 us
    all_to_all x1, blocking collectives, body(): prior = lax.all_to_all(priors, BLOCKS, 0, 0, tiled=True).reshape(STATE)  12.2 us
    unnamed x42, local copies, waits for them, and re-layouts  6.95 us
    pallas_call x1, Pallas kernels, body(): call(early_kernel, [(SQUARE, F32), wide, (SQUARE, BF)], 3, 1 << 33, 7, [p...  6.77 us
    ppermute x3, waiting for transfers between devices, swap_cores(): return lax.ppermute(x, 'core', [(0, 1), (1, 0)])  6.2 us
    pallas_call x1, Pallas kernels, body(): call(post_kernel, [(SQUARE, BF), (SQUARE, F32), (SQUARE, F32), TOKEN], 5,...  4.37 us
  transfers between devices with their start and end apart: 31, of which 11 were waited for; matrix products, arithmetic and copies ran while one was open for 0% of the time, Pallas kernels for 15%

commit v1 on v0

--- a/solution.py
+++ b/solution.py
@@ -38,8 +38,8 @@
     return pl.ds(pl.multiple_of(h * HEAD_DIM, HEAD_DIM), HEAD_DIM)
 
 
-def each(count, step):
-    lax.fori_loop(0, count, lambda i, carry: (step(i), carry)[1], 0)
+def each(count, step, unroll=1):
+    lax.fori_loop(0, count, lambda i, carry: (step(i), carry)[1], 0, unroll=unroll)
 
 
 def causal_mask():
@@ -97,7 +97,7 @@
         gated = (att * inverse * gain_ref[:, cols]).astype(BF)
         gated_ref[cols, :] = gated.T
 
-    each(HEADS, step)
+    each(HEADS, step, 2)
 
 
 def is_same():
@@ -134,26 +134,34 @@
             k = jnp.where(n == i, ORDER[i], k)
         return k
 
-    def fetch(even, k):
+    def fetch(even, k, slot):
         mine = jnp.logical_not(jnp.logical_xor(same, even))
         y = row_of(k)
 
         @pl.when(mine)
         def _():
-            weight_ref[...] = wm_ref[y].reshape(SQUARE)
+            weight_ref[slot] = wm_ref[y].reshape(SQUARE)
 
         @pl.when(jnp.logical_not(mine))
         def _():
-            weight_ref[...] = wo_ref[y].reshape(SQUARE)
-
-    def step(n):
-        slot = jnp.where(n < 3, n, n + 1)
-        part_ref[slot] = dot(gated_ref[...], rows[n], NN).astype(BF)
-        fetch(n < 3, offset(n))
-        sum_ref[...] += dot(rows[n], weight_ref[...], NN)
-
-    each(7, step)
-    fetch(jnp.bool_(True), jnp.int32(4))
+            weight_ref[slot] = wo_ref[y].reshape(SQUARE)
+
+    def part(n):
+        part_ref[jnp.where(n < 3, n, n + 1)] = dot(gated_ref[...], rows[n], NN).astype(BF)
+
+    def step(i):
+        n = 2 * i
+        for m in range(2):
+            fetch(n + m < 3, offset(n + m), m)
+            part(n + m)
+        first = dot(rows[n], weight_ref[0], NN)
+        sum_ref[...] += first + dot(rows[n + 1], weight_ref[1], NN)
+
+    each(3, step)
+    fetch(jnp.bool_(False), jnp.int32(ORDER[6]), 0)
+    part(jnp.int32(6))
+    sum_ref[...] += dot(rows[6], weight_ref[0], NN)
+    fetch(jnp.bool_(True), jnp.int32(4), 0)
 
 
 def last_kernel(low_ref, high_ref, gated_ref, part_ref, last_ref, other_ref):
@@ -177,16 +185,17 @@
 
 
 def grad_kernel(
-    low_ref, high_ref, weight_ref, sum_ref, q_ref, att_ref, gain_ref, ga_ref, send_ref, acc
+    low_ref, high_ref, weight_ref, sum_ref, q_ref, att_ref, gain_ref, ga_ref, send_ref, token_ref, acc
 ):
+    token_ref[...] = jnp.zeros(TOKEN[0], F32)
     half = TOKENS // 2
-    acc[0:half] = sum_ref[0:half] + dot(low_ref[...], weight_ref[...], NN)
-    acc[half:TOKENS] = sum_ref[half:TOKENS] + dot(high_ref[...], weight_ref[...], NN)
+    acc[0:half] = sum_ref[0:half] + dot(low_ref[...], weight_ref[0], NN)
+    acc[half:TOKENS] = sum_ref[half:TOKENS] + dot(high_ref[...], weight_ref[0], NN)
     grad_rows(acc, q_ref, att_ref, gain_ref, ga_ref, send_ref)
 
 
 def combine_kernel(
-    part_ref, got_ref, last_ref, own_ref, up_ref, down_ref, low_ref, high_ref, rows
+    after_ref, part_ref, got_ref, last_ref, own_ref, up_ref, down_ref, low_ref, high_ref, rows
 ):
     place = lax.axis_index("dp")
     same = is_same()
@@ -310,7 +319,7 @@
         send_ref[span(h)] = dot(q_ref[:, span(h)], grad, TN).astype(BF)
         return sums
 
-    sums = lax.fori_loop(0, HEADS, step, jnp.zeros((16, HEAD_DIM), F32))
+    sums = lax.fori_loop(0, HEADS, step, jnp.zeros((16, HEAD_DIM), F32), unroll=2)
     send_ref[base:] = sums.astype(BF)
 
 
@@ -367,7 +376,7 @@
         kg_ref[:, cols] = (kp_ref[:, cols] + dot(v_ref[:, cols], later, NT)).astype(BF)
         vg_ref[:, cols] = (vp_ref[:, cols] + dot(k_ref[:, cols], later, NN)).astype(BF)
 
-    each(HEADS, step)
+    each(HEADS, step, 2)
     gain = resum([r[base:] for r in (own, u1, u2, u3)])
     gain_ref[...] = (gain[0:4] + gain[4:8]) * SCALE
 
@@ -429,7 +438,7 @@
     wide = ((8, WIDTH, WIDTH), BF)
     partial_sum, parts, weight_last = call(
         early_kernel,
-        [(SQUARE, F32), wide, (SQUARE, BF)],
+        [(SQUARE, F32), wide, ((2, WIDTH, WIDTH), BF)],
         3,
         1 << 33,
         7,
@@ -438,9 +447,9 @@
     last, other = call(last_kernel, [(SQUARE, BF), ((4, WIDTH, WIDTH), BF)], 4, 1 << 29)(
         last_low, last_high, gated, parts
     )
-    ga, send = call(
+    ga, send, grad_token = call(
         grad_kernel,
-        [(SQUARE, BF), (STATE_GAIN, BF)],
+        [(SQUARE, BF), (STATE_GAIN, BF), TOKEN],
         7,
         1 << 30,
         0,
@@ -450,11 +459,11 @@
     part, up, down, low, high = call(
         combine_kernel,
         [quarter, quarter, quarter, eighth, eighth],
-        3,
+        4,
         1 << 20,
         0,
         [pltpu.VMEM(SQUARE, BF)],
-    )(parts, swap_cores(other), last)
+    )(grad_token, parts, swap_cores(other), last)
     total, after = call(row_back_kernel, [(STATE_GAIN, BF), (STATE, F32)], 4, 1 << 22)(
         send, *[shift(send, "dp", 4, -k) for k in (1, 2, 3)]
     )

time: 128 us -> 126 us (0.984)
  Pallas kernels: 25.3 us -> 22.8 us
    ppermute x28, waiting for transfers between devices: 16.1 us -> 18.6 us  [shift(): return lax.ppermute(x, axis, pairs)]
    ppermute x3, waiting for transfers between devices: 6.2 us -> 4.26 us  [swap_cores(): return lax.ppermute(x, 'core', [(0, 1), (1, 0)])]
    pallas_call x3, Pallas kernels: 9.81 us -> 8.25 us  [the longest x1 5.64 us: body(): call(early_kernel, [(SQUARE, F32), wide, ((2, WIDTH, WIDTH), BF)], 3, 1 <...]
  transfers between devices with their start and end apart: 31 -> 31, of which waited for: 11 -> 12; matrix products, arithmetic and copies ran while one was open for 0% -> 0% of each run, Pallas kernels for 15% -> 13%
where the time goes in v1:
time: 126 us
  starting transfers between devices  44.9 us (36%)
  blocking collectives  26.7 us (21%)
  waiting for transfers between devices  22.9 us (18%)
  Pallas kernels  22.8 us (18%)
  local copies, waits for them, and re-layouts  7.23 us (6%)
    ppermute x28, starting transfers between devices, shift(): return lax.ppermute(x, axis, pairs)  44.7 us
    ppermute x28, waiting for transfers between devices, shift(): return lax.ppermute(x, axis, pairs)  18.6 us
    all_to_all x1, blocking collectives, body(): states = lax.all_to_all(state, BLOCKS, 0, 0, tiled=True)  14.5 us
    all_to_all x1, blocking collectives, body(): prior = lax.all_to_all(priors, BLOCKS, 0, 0, tiled=True).reshape(STATE)  12.2 us
    unnamed x42, local copies, waits for them, and re-layouts  7.23 us
    pallas_call x1, Pallas kernels, body(): call(early_kernel, [(SQUARE, F32), wide, ((2, WIDTH, WIDTH), BF)], 3, 1 <...  5.64 us
    pallas_call x1, Pallas kernels, body(): call(post_kernel, [(SQUARE, BF), (SQUARE, F32), (SQUARE, F32), TOKEN], 5,...  4.37 us
    ppermute x3, waiting for transfers between devices, swap_cores(): return lax.ppermute(x, 'core', [(0, 1), (1, 0)])  4.26 us
  transfers between devices with their start and end apart: 31, of which 12 were waited for; matrix products, arithmetic and copies ran while one was open for 0% of the time, Pallas kernels for 13%

profile of v1, /device:TPU:6, one launch (start us, length us, event | category | flops | bytes accessed | tf_op | source)
XLA Modules:
  0.0 125.5 jit_solution(14815182494100100963)
XLA Ops:
  0.6 2.0 %collective-permute-start = (bf16[512,512]{1,0:T(8,128)(2,1)}, bf16[512,512]{1,0:T(8,128)(2,1)S(1)}, u32[]{:S(2)}, u32[]{:S(2)}) collective-permute-start(bf16[512,512]{1,0:T(8,128)(2,1)} %refs_0_.1), channel_id=1, source_target_pairs={{0,4},{4,8},{8,12},{12,16},{16,20},{20,24},{24,28},{28,0},{1,5},{5... | collective-permute-start | bytes 1572872 | tf_op jit(solution)/shard_map/ppermute | solution.py:393
  2.6 4.0 %collective-permute-start.1 = (bf16[512,512]{1,0:T(8,128)(2,1)}, bf16[512,512]{1,0:T(8,128)(2,1)S(1)}, u32[]{:S(2)}, u32[]{:S(2)}) collective-permute-start(bf16[512,512]{1,0:T(8,128)(2,1)} %refs_0_.1), channel_id=1, source_target_pairs={{0,28},{4,0},{8,4},{12,8},{16,12},{20,16},{24,20},{28,24},{1,29},{... | collective-permute-start | bytes 1572872 | tf_op jit(solution)/shard_map/ppermute | solution.py:393
  6.7 3.2 %collective-permute-start.3 = (bf16[128,512]{1,0:T(8,128)(2,1)}, bf16[128,512]{1,0:T(8,128)(2,1)S(1)}, u32[]{:S(2)}, u32[]{:S(2)}) collective-permute-start(bf16[128,512]{1,0:T(8,128)(2,1)} %own_ref.1), channel_id=1, source_target_pairs={{0,128},{64,192},{128,0},{192,64},{1,129},{65,193},{129,1},{193,65... | collective-permute-start | bytes 393224 | tf_op jit(solution)/shard_map/ppermute | solution.py:393
  10.5 2.6 %collective-permute-start.4 = (bf16[128,512]{1,0:T(8,128)(2,1)}, bf16[128,512]{1,0:T(8,128)(2,1)S(1)}, u32[]{:S(2)}, u32[]{:S(2)}) collective-permute-start(bf16[128,512]{1,0:T(8,128)(2,1)} %own_ref.1), channel_id=1, source_target_pairs={{0,192},{64,0},{128,64},{192,128},{1,193},{65,1},{129,65},{193,129... | collective-permute-start | bytes 393224 | tf_op jit(solution)/shard_map/ppermute | solution.py:393
  16.7 2.0 %collective-permute-done.after1_ref.refs_0_ = bf16[512,512]{1,0:T(8,128)(2,1)S(1)} collective-permute-done((bf16[512,512]{1,0:T(8,128)(2,1)}, bf16[512,512]{1,0:T(8,128)(2,1)S(1)}, u32[]{:S(2)}, u32[]{:S(2)}) %collective-permute-start) | collective-permute-done | bytes 524320 | tf_op jit(solution)/shard_map/ppermute | solution.py:393
  22.0 3.2 %collective-permute-start.6 = (bf16[512,512]{1,0:T(8,128)(2,1)}, bf16[512,512]{1,0:T(8,128)(2,1)S(1)}, u32[]{:S(2)}, u32[]{:S(2)}) collective-permute-start(bf16[512,512]{1,0:T(8,128)(2,1)} %get-tuple-element.56.refs_2_), channel_id=1, source_target_pairs={{0,28},{4,0},{8,4},{12,8},{16,12},{20,16},{24,20},{28,24},{1,29},{... | collective-permute-start | bytes 1572872 | tf_op jit(solution)/shard_map/ppermute | solution.py:393
  26.1 2.4 %collective-permute-start.9 = (bf16[4,128,512]{2,1,0:T(8,128)(2,1)}, bf16[4,128,512]{2,1,0:T(8,128)(2,1)S(1)}, u32[]{:S(2)}, u32[]{:S(2)}) collective-permute-start(bf16[4,128,512]{2,1,0:T(8,128)(2,1)} %get-tuple-element.60.own_ref), channel_id=1, source_target_pairs={{0,1},{1,2},{2,3},{3,0},{4,5},{5,6},{6,7},{7,4},{8,9},{9,10},{10,1... | collective-permute-start | bytes 1572872 | tf_op jit(solution)/shard_map/ppermute | solution.py:393
  28.5 14.5 %all_to_all.10.in_ref = bf16[32,16,128]{2,1,0:T(8,128)(2,1)S(1)} all-to-all(bf16[32,16,128]{2,1,0:T(8,128)(2,1)S(1)} %get-tuple-element.50), channel_id=1, replica_groups=mesh['y'=4,'core'=2,'tp'=8,'dp'=4] {'y','core','dp'}, dimensions={0} | all-to-all | bytes 262144 | tf_op jit(solution)/shard_map/all_to_all | solution.py:405
  45.4 3.2 %collective-permute-start.8 = (bf16[512,512]{1,0:T(8,128)(2,1)}, bf16[512,512]{1,0:T(8,128)(2,1)S(1)}, u32[]{:S(2)}, u32[]{:S(2)}) collective-permute-start(bf16[512,512]{1,0:T(8,128)(2,1)} %get-tuple-element.59.refs_4_), channel_id=1, source_target_pairs={{0,28},{4,0},{8,4},{12,8},{16,12},{20,16},{24,20},{28,24},{1,29},{... | collective-permute-start | bytes 1572872 | tf_op jit(solution)/shard_map/ppermute | solution.py:393
  48.6 3.2 %collective-permute-start.11 = (bf16[2,128,512]{2,1,0:T(8,128)(2,1)}, bf16[2,128,512]{2,1,0:T(8,128)(2,1)S(1)}, u32[]{:S(2)}, u32[]{:S(2)}) collective-permute-start(bf16[2,128,512]{2,1,0:T(8,128)(2,1)} %copy-done.20), channel_id=1, source_target_pairs={{0,1},{1,2},{2,3},{3,0},{4,5},{5,6},{6,7},{7,4},{8,9},{9,10},{10,1... | collective-permute-start | bytes 786440 | tf_op jit(solution)/shard_map/ppermute | solution.py:393
  51.8 12.2 %all_to_all.11 = bf16[32,16,128]{2,1,0:T(8,128)(2,1)S(1)} all-to-all(bf16[32,16,128]{2,1,0:T(8,128)(2,1)S(1)} %get-tuple-element.51), channel_id=1, replica_groups=mesh['y'=4,'core'=2,'tp'=8,'dp'=4] {'y','core','dp'}, dimensions={0} | all-to-all | bytes 262144 | tf_op jit(solution)/shard_map/all_to_all | solution.py:415
  65.1 1.9 %shard_map.103 = (f32[512,512]{1,0:T(8,128)S(1)}, bf16[512,512]{1,0:T(8,128)(2,1)S(1)}) custom-call(bf16[512,512]{1,0:T(8,128)(2,1)S(1)} %copy-done.12, bf16[512,512]{1,0:T(8,128)(2,1)S(1)} %copy-done.1, bf16[512,512]{1,0:T(8,128)(2,1)S(1)} %copy-done.3, f32[1,512]{1,0:T(1,128)S(1)} %bitcast.5, bf16[512,128]{1,0:T(8,128)(2,1)S(1)} %bitcast.3), custom_call_target="tpu_custom_call" | custom-call | flops 1073741824 | bytes 4194304 | tf_op jit(solution)/shard_map/pallas_call | solution.py:418
  68.6 3.2 %collective-permute-start.14 = (bf16[256,512]{1,0:T(8,128)(2,1)S(1)}, bf16[256,512]{1,0:T(8,128)(2,1)S(1)}, u32[]{:S(2)}, u32[]{:S(2)}) collective-permute-start(bf16[256,512]{1,0:T(8,128)(2,1)S(1)} %get-tuple-element.64), channel_id=1, source_target_pairs={{0,28},{4,0},{8,4},{12,8},{16,12},{20,16},{24,20},{28,24},{1,29},{... | collective-permute-start | bytes 786440 | tf_op jit(solution)/shard_map/ppermute | solution.py:393
  72.7 5.6 %shard_map.109 = (f32[512,512]{1,0:T(8,128)S(1)}, bf16[8,512,512]{2,1,0:T(8,128)(2,1)S(1)}, bf16[2,512,512]{2,1,0:T(8,128)(2,1)S(1)}) custom-call(bf16[512,512]{1,0:T(8,128)(2,1)S(1)} %copy-done.19, bf16[512,512]{1,0:T(8,128)(2,1)S(1)} %copy-done.5, bf16[512,512]{1,0:T(8,128)(2,1)S(1)} %copy-done.7, bf16[512,512]{1,0:T(8,128)(2,1)S(1)} %copy-done.9, ...), custom_call_target="tpu_custom_call" | custom-call | flops 8589934592 | bytes 4194304 | tf_op jit(solution)/shard_map/pallas_call | solution.py:439
  81.2 2.1 %collective-permute-done.16.got_ref = bf16[4,512,512]{2,1,0:T(8,128)(2,1)S(1)} collective-permute-done((bf16[4,512,512]{2,1,0:T(8,128)(2,1)S(1)}, bf16[4,512,512]{2,1,0:T(8,128)(2,1)S(1)}, u32[]{:S(2)}, u32[]{:S(2)}) %collective-permute-start.16) | collective-permute-done | bytes 2097184 | tf_op jit(solution)/shard_map/ppermute | solution.py:397
  84.2 1.7 %collective-permute-start.20 = (bf16[1024,128]{1,0:T(8,128)(2,1)S(1)}, bf16[1024,128]{1,0:T(8,128)(2,1)S(1)}, u32[]{:S(2)}, u32[]{:S(2)}) collective-permute-start(bf16[1024,128]{1,0:T(8,128)(2,1)S(1)} %get-tuple-element.81), channel_id=1, source_target_pairs={{0,1},{1,2},{2,3},{3,0},{4,5},{5,6},{6,7},{7,4},{8,9},{9,10},{10,1... | collective-permute-start | bytes 786440 | tf_op jit(solution)/shard_map/ppermute | solution.py:393
  86.3 2.9 %collective-permute-start.19 = (bf16[528,128]{1,0:T(8,128)(2,1)S(1)}, bf16[528,128]{1,0:T(8,128)(2,1)S(1)}, u32[]{:S(2)}, u32[]{:S(2)}) collective-permute-start(bf16[528,128]{1,0:T(8,128)(2,1)S(1)} %get-tuple-element.77.own_ref), channel_id=1, source_target_pairs={{0,1},{1,2},{2,3},{3,0},{4,5},{5,6},{6,7},{7,4},{8,9},{9,10},{10,1... | collective-permute-start | bytes 405512 | tf_op jit(solution)/shard_map/ppermute | solution.py:393
  90.1 6.3 %collective-permute-done.19.r3_ref = bf16[528,128]{1,0:T(8,128)(2,1)S(1)} collective-permute-done((bf16[528,128]{1,0:T(8,128)(2,1)S(1)}, bf16[528,128]{1,0:T(8,128)(2,1)S(1)}, u32[]{:S(2)}, u32[]{:S(2)}) %collective-permute-start.19) | collective-permute-done | bytes 135200 | tf_op jit(solution)/shard_map/ppermute | solution.py:393
  98.0 3.1 %collective-permute-done.17.r1_ref = bf16[528,128]{1,0:T(8,128)(2,1)S(1)} collective-permute-done((bf16[528,128]{1,0:T(8,128)(2,1)S(1)}, bf16[528,128]{1,0:T(8,128)(2,1)S(1)}, u32[]{:S(2)}, u32[]{:S(2)}) %collective-permute-start.17) | collective-permute-done | bytes 135200 | tf_op jit(solution)/shard_map/ppermute | solution.py:393
  101.8 1.7 %collective-permute-start.23 = (bf16[4,512,128]{2,1,0:T(8,128)(2,1)S(1)}, bf16[4,512,128]{2,1,0:T(8,128)(2,1)S(1)}, u32[]{:S(2)}, u32[]{:S(2)}) collective-permute-start(bf16[4,512,128]{2,1,0:T(8,128)(2,1)S(1)} %get-tuple-element.84), channel_id=1, source_target_pairs={{0,3},{1,0},{2,1},{3,2},{4,7},{5,4},{6,5},{7,6},{8,11},{9,8},{10,9... | collective-permute-start | bytes 1572872 | tf_op jit(solution)/shard_map/ppermute | solution.py:393
  105.6 2.0 %collective-permute-start.26 = (bf16[528,128]{1,0:T(8,128)(2,1)S(1)}, bf16[528,128]{1,0:T(8,128)(2,1)S(1)}, u32[]{:S(2)}, u32[]{:S(2)}) collective-permute-start(bf16[528,128]{1,0:T(8,128)(2,1)S(1)} %shard_map.117.own), channel_id=1, source_target_pairs={{0,128},{64,192},{128,0},{192,64},{1,129},{65,193},{129,1},{193,65... | collective-permute-start | bytes 405512 | tf_op jit(solution)/shard_map/ppermute | solution.py:393
  108.9 4.4 %shard_map.111 = (bf16[512,512]{1,0:T(8,128)(2,1)}, f32[512,512]{1,0:T(8,128)S(1)}, f32[512,512]{1,0:T(8,128)S(1)}, f32[8,128]{1,0:T(8,128)S(1)}) custom-call(bf16[512,512]{1,0:T(8,128)(2,1)S(1)} %copy-done.13, bf16[512,512]{1,0:T(8,128)(2,1)S(1)} %copy-done.1, bf16[512,512]{1,0:T(8,128)(2,1)S(1)} %copy-done.3, ...), custom_call_target="tpu_custom_call" | custom-call | flops 2147483648 | bytes 4194304 | tf_op jit(solution)/shard_map/pallas_call | solution.py:473
  116.8 1.9 %collective-permute-start.29 = (bf16[512,128]{1,0:T(8,128)(2,1)S(1)}, bf16[512,128]{1,0:T(8,128)(2,1)S(1)}, u32[]{:S(2)}, u32[]{:S(2)}) collective-permute-start(bf16[512,128]{1,0:T(8,128)(2,1)S(1)} %get-tuple-element.94), channel_id=1, source_target_pairs={{0,128},{64,192},{128,0},{192,64},{1,129},{65,193},{129,1},{193,65... | collective-permute-start | bytes 393224 | tf_op jit(solution)/shard_map/ppermute | solution.py:393
  121.8 2.0 %collective-permute-done.28.r1_ref = bf16[512,128]{1,0:T(8,128)(2,1)S(1)} collective-permute-done((bf16[512,128]{1,0:T(8,128)(2,1)S(1)}, bf16[512,128]{1,0:T(8,128)(2,1)S(1)}, u32[]{:S(2)}, u32[]{:S(2)}) %collective-permute-start.28) | collective-permute-done | bytes 131104 | tf_op jit(solution)/shard_map/ppermute | solution.py:393
  (101 shorter events, 33.2 us)
Async XLA Ops:
  0.6 18.1 %collective-permute-start = (bf16[512,512]{1,0:T(8,128)(2,1)}, bf16[512,512]{1,0:T(8,128)(2,1)S(1)}, u32[]{:S(2)}, u32[]{:S(2)}) collective-permute-start(bf16[512,512]{1,0:T(8,128)(2,1)} %refs_0_.1), channel_id=1, source_target_pairs={{0,4},{4,8},{8,12},{12,16},{16,20},{20,24},{24,28},{28,0},{1,5},{5... | collective-permute-start | bytes 1572872 | tf_op jit(solution)/shard_map/ppermute | solution.py:393
  2.6 16.1 %collective-permute-start.1 = (bf16[512,512]{1,0:T(8,128)(2,1)}, bf16[512,512]{1,0:T(8,128)(2,1)S(1)}, u32[]{:S(2)}, u32[]{:S(2)}) collective-permute-start(bf16[512,512]{1,0:T(8,128)(2,1)} %refs_0_.1), channel_id=1, source_target_pairs={{0,28},{4,0},{8,4},{12,8},{16,12},{20,16},{24,20},{28,24},{1,29},{... | collective-permute-start | bytes 1572872 | tf_op jit(solution)/shard_map/ppermute | solution.py:393
  6.7 10.0 %collective-permute-start.3 = (bf16[128,512]{1,0:T(8,128)(2,1)}, bf16[128,512]{1,0:T(8,128)(2,1)S(1)}, u32[]{:S(2)}, u32[]{:S(2)}) collective-permute-start(bf16[128,512]{1,0:T(8,128)(2,1)} %own_ref.1), channel_id=1, source_target_pairs={{0,128},{64,192},{128,0},{192,64},{1,129},{65,193},{129,1},{193,65... | collective-permute-start | bytes 393224 | tf_op jit(solution)/shard_map/ppermute | solution.py:393
  21.9 21.7 %collective-permute-start.5 = (bf16[512,512]{1,0:T(8,128)(2,1)}, bf16[512,512]{1,0:T(8,128)(2,1)S(1)}, u32[]{:S(2)}, u32[]{:S(2)}) collective-permute-start(bf16[512,512]{1,0:T(8,128)(2,1)} %get-tuple-element.55.refs_1_), channel_id=1, source_target_pairs={{0,4},{4,8},{8,12},{12,16},{16,20},{20,24},{24,28},{28,0},{1,5},{5... | collective-permute-start | bytes 1572872 | tf_op jit(solution)/shard_map/ppermute | solution.py:393
  22.0 21.6 %collective-permute-start.6 = (bf16[512,512]{1,0:T(8,128)(2,1)}, bf16[512,512]{1,0:T(8,128)(2,1)S(1)}, u32[]{:S(2)}, u32[]{:S(2)}) collective-permute-start(bf16[512,512]{1,0:T(8,128)(2,1)} %get-tuple-element.56.refs_2_), channel_id=1, source_target_pairs={{0,28},{4,0},{8,4},{12,8},{16,12},{20,16},{24,20},{28,24},{1,29},{... | collective-permute-start | bytes 1572872 | tf_op jit(solution)/shard_map/ppermute | solution.py:393
  25.2 18.4 %collective-permute-start.10 = (bf16[4,128,512]{2,1,0:T(8,128)(2,1)}, bf16[4,128,512]{2,1,0:T(8,128)(2,1)S(1)}, u32[]{:S(2)}, u32[]{:S(2)}) collective-permute-start(bf16[4,128,512]{2,1,0:T(8,128)(2,1)} %get-tuple-element.60.own_ref), channel_id=1, source_target_pairs={{0,3},{1,0},{2,1},{3,2},{4,7},{5,4},{6,5},{7,6},{8,11},{9,8},{10,9... | collective-permute-start | bytes 1572872 | tf_op jit(solution)/shard_map/ppermute | solution.py:393
  26.1 17.6 %collective-permute-start.9 = (bf16[4,128,512]{2,1,0:T(8,128)(2,1)}, bf16[4,128,512]{2,1,0:T(8,128)(2,1)S(1)}, u32[]{:S(2)}, u32[]{:S(2)}) collective-permute-start(bf16[4,128,512]{2,1,0:T(8,128)(2,1)} %get-tuple-element.60.own_ref), channel_id=1, source_target_pairs={{0,1},{1,2},{2,3},{3,0},{4,5},{5,6},{6,7},{7,4},{8,9},{9,10},{10,1... | collective-permute-start | bytes 1572872 | tf_op jit(solution)/shard_map/ppermute | solution.py:393
  45.4 21.6 %collective-permute-start.7 = (bf16[512,512]{1,0:T(8,128)(2,1)}, bf16[512,512]{1,0:T(8,128)(2,1)S(1)}, u32[]{:S(2)}, u32[]{:S(2)}) collective-permute-start(bf16[512,512]{1,0:T(8,128)(2,1)} %get-tuple-element.58.refs_3_), channel_id=1, source_target_pairs={{0,4},{4,8},{8,12},{12,16},{16,20},{20,24},{24,28},{28,0},{1,5},{5... | collective-permute-start | bytes 1572872 | tf_op jit(solution)/shard_map/ppermute | solution.py:393
  45.4 21.7 %collective-permute-start.8 = (bf16[512,512]{1,0:T(8,128)(2,1)}, bf16[512,512]{1,0:T(8,128)(2,1)S(1)}, u32[]{:S(2)}, u32[]{:S(2)}) collective-permute-start(bf16[512,512]{1,0:T(8,128)(2,1)} %get-tuple-element.59.refs_4_), channel_id=1, source_target_pairs={{0,28},{4,0},{8,4},{12,8},{16,12},{20,16},{24,20},{28,24},{1,29},{... | collective-permute-start | bytes 1572872 | tf_op jit(solution)/shard_map/ppermute | solution.py:393
  48.6 18.4 %collective-permute-start.11 = (bf16[2,128,512]{2,1,0:T(8,128)(2,1)}, bf16[2,128,512]{2,1,0:T(8,128)(2,1)S(1)}, u32[]{:S(2)}, u32[]{:S(2)}) collective-permute-start(bf16[2,128,512]{2,1,0:T(8,128)(2,1)} %copy-done.20), channel_id=1, source_target_pairs={{0,1},{1,2},{2,3},{3,0},{4,5},{5,6},{6,7},{7,4},{8,9},{9,10},{10,1... | collective-permute-start | bytes 786440 | tf_op jit(solution)/shard_map/ppermute | solution.py:393
  51.8 15.2 %collective-permute-start.12 = (bf16[2,128,512]{2,1,0:T(8,128)(2,1)S(1)}, bf16[2,128,512]{2,1,0:T(8,128)(2,1)S(1)}, u32[]{:S(2)}, u32[]{:S(2)}) collective-permute-start(bf16[2,128,512]{2,1,0:T(8,128)(2,1)S(1)} %get-tuple-element.62), channel_id=1, source_target_pairs={{0,3},{1,0},{2,1},{3,2},{4,7},{5,4},{6,5},{7,6},{8,11},{9,8},{10,9... | collective-permute-start | bytes 786440 | tf_op jit(solution)/shard_map/ppermute | solution.py:393
  68.5 9.9 %collective-permute-start.13 = (bf16[256,512]{1,0:T(8,128)(2,1)S(1)}, bf16[256,512]{1,0:T(8,128)(2,1)S(1)}, u32[]{:S(2)}, u32[]{:S(2)}) collective-permute-start(bf16[256,512]{1,0:T(8,128)(2,1)S(1)} %get-tuple-element.63), channel_id=1, source_target_pairs={{0,4},{4,8},{8,12},{12,16},{16,20},{20,24},{24,28},{28,0},{1,5},{5... | collective-permute-start | bytes 786440 | tf_op jit(solution)/shard_map/ppermute | solution.py:393
  68.6 9.8 %collective-permute-start.14 = (bf16[256,512]{1,0:T(8,128)(2,1)S(1)}, bf16[256,512]{1,0:T(8,128)(2,1)S(1)}, u32[]{:S(2)}, u32[]{:S(2)}) collective-permute-start(bf16[256,512]{1,0:T(8,128)(2,1)S(1)} %get-tuple-element.64), channel_id=1, source_target_pairs={{0,28},{4,0},{8,4},{12,8},{16,12},{20,16},{24,20},{28,24},{1,29},{... | collective-permute-start | bytes 786440 | tf_op jit(solution)/shard_map/ppermute | solution.py:393
  84.2 17.0 %collective-permute-start.20 = (bf16[1024,128]{1,0:T(8,128)(2,1)S(1)}, bf16[1024,128]{1,0:T(8,128)(2,1)S(1)}, u32[]{:S(2)}, u32[]{:S(2)}) collective-permute-start(bf16[1024,128]{1,0:T(8,128)(2,1)S(1)} %get-tuple-element.81), channel_id=1, source_target_pairs={{0,1},{1,2},{2,3},{3,0},{4,5},{5,6},{6,7},{7,4},{8,9},{9,10},{10,1... | collective-permute-start | bytes 786440 | tf_op jit(solution)/shard_map/ppermute | solution.py:393
  86.0 15.3 %collective-permute-start.21 = (bf16[1024,128]{1,0:T(8,128)(2,1)S(1)}, bf16[1024,128]{1,0:T(8,128)(2,1)S(1)}, u32[]{:S(2)}, u32[]{:S(2)}) collective-permute-start(bf16[1024,128]{1,0:T(8,128)(2,1)S(1)} %get-tuple-element.82), channel_id=1, source_target_pairs={{0,3},{1,0},{2,1},{3,2},{4,7},{5,4},{6,5},{7,6},{8,11},{9,8},{10,9... | collective-permute-start | bytes 786440 | tf_op jit(solution)/shard_map/ppermute | solution.py:393
  86.3 10.0 %collective-permute-start.19 = (bf16[528,128]{1,0:T(8,128)(2,1)S(1)}, bf16[528,128]{1,0:T(8,128)(2,1)S(1)}, u32[]{:S(2)}, u32[]{:S(2)}) collective-permute-start(bf16[528,128]{1,0:T(8,128)(2,1)S(1)} %get-tuple-element.77.own_ref), channel_id=1, source_target_pairs={{0,1},{1,2},{2,3},{3,0},{4,5},{5,6},{6,7},{7,4},{8,9},{9,10},{10,1... | collective-permute-start | bytes 405512 | tf_op jit(solution)/shard_map/ppermute | solution.py:393
  89.2 8.8 %collective-permute-start.18 = (bf16[528,128]{1,0:T(8,128)(2,1)S(1)}, bf16[528,128]{1,0:T(8,128)(2,1)S(1)}, u32[]{:S(2)}, u32[]{:S(2)}) collective-permute-start(bf16[528,128]{1,0:T(8,128)(2,1)S(1)} %get-tuple-element.77.own_ref), channel_id=1, source_target_pairs={{0,2},{1,3},{2,0},{3,1},{4,6},{5,7},{6,4},{7,5},{8,10},{9,11},{10,... | collective-permute-start | bytes 405512 | tf_op jit(solution)/shard_map/ppermute | solution.py:393
  89.2 11.9 %collective-permute-start.17 = (bf16[528,128]{1,0:T(8,128)(2,1)S(1)}, bf16[528,128]{1,0:T(8,128)(2,1)S(1)}, u32[]{:S(2)}, u32[]{:S(2)}) collective-permute-start(bf16[528,128]{1,0:T(8,128)(2,1)S(1)} %get-tuple-element.77.own_ref), channel_id=1, source_target_pairs={{0,3},{1,0},{2,1},{3,2},{4,7},{5,4},{6,5},{7,6},{8,11},{9,8},{10,9... | collective-permute-start | bytes 405512 | tf_op jit(solution)/shard_map/ppermute | solution.py:393
  101.4 12.9 %collective-permute-start.22 = (bf16[4,512,128]{2,1,0:T(8,128)(2,1)S(1)}, bf16[4,512,128]{2,1,0:T(8,128)(2,1)S(1)}, u32[]{:S(2)}, u32[]{:S(2)}) collective-permute-start(bf16[4,512,128]{2,1,0:T(8,128)(2,1)S(1)} %get-tuple-element.83), channel_id=1, source_target_pairs={{0,1},{1,2},{2,3},{3,0},{4,5},{5,6},{6,7},{7,4},{8,9},{9,10},{10,1... | collective-permute-start | bytes 1572872 | tf_op jit(solution)/shard_map/ppermute | solution.py:393
  101.8 14.1 %collective-permute-start.23 = (bf16[4,512,128]{2,1,0:T(8,128)(2,1)S(1)}, bf16[4,512,128]{2,1,0:T(8,128)(2,1)S(1)}, u32[]{:S(2)}, u32[]{:S(2)}) collective-permute-start(bf16[4,512,128]{2,1,0:T(8,128)(2,1)S(1)} %get-tuple-element.84), channel_id=1, source_target_pairs={{0,3},{1,0},{2,1},{3,2},{4,7},{5,4},{6,5},{7,6},{8,11},{9,8},{10,9... | collective-permute-start | bytes 1572872 | tf_op jit(solution)/shard_map/ppermute | solution.py:393
  104.9 13.9 %collective-permute-start.27 = (bf16[528,128]{1,0:T(8,128)(2,1)S(1)}, bf16[528,128]{1,0:T(8,128)(2,1)S(1)}, u32[]{:S(2)}, u32[]{:S(2)}) collective-permute-start(bf16[528,128]{1,0:T(8,128)(2,1)S(1)} %shard_map.117.own), channel_id=1, source_target_pairs={{0,64},{64,128},{128,192},{192,0},{1,65},{65,129},{129,193},{193,1... | collective-permute-start | bytes 405512 | tf_op jit(solution)/shard_map/ppermute | solution.py:393
  105.6 14.6 %collective-permute-start.26 = (bf16[528,128]{1,0:T(8,128)(2,1)S(1)}, bf16[528,128]{1,0:T(8,128)(2,1)S(1)}, u32[]{:S(2)}, u32[]{:S(2)}) collective-permute-start(bf16[528,128]{1,0:T(8,128)(2,1)S(1)} %shard_map.117.own), channel_id=1, source_target_pairs={{0,128},{64,192},{128,0},{192,64},{1,129},{65,193},{129,1},{193,65... | collective-permute-start | bytes 405512 | tf_op jit(solution)/shard_map/ppermute | solution.py:393
  107.6 12.6 %collective-permute-start.25 = (bf16[528,128]{1,0:T(8,128)(2,1)S(1)}, bf16[528,128]{1,0:T(8,128)(2,1)S(1)}, u32[]{:S(2)}, u32[]{:S(2)}) collective-permute-start(bf16[528,128]{1,0:T(8,128)(2,1)S(1)} %shard_map.117.own), channel_id=1, source_target_pairs={{0,192},{64,0},{128,64},{192,128},{1,193},{65,1},{129,65},{193,129... | collective-permute-start | bytes 405512 | tf_op jit(solution)/shard_map/ppermute | solution.py:393
  116.1 7.7 %collective-permute-start.28 = (bf16[512,128]{1,0:T(8,128)(2,1)S(1)}, bf16[512,128]{1,0:T(8,128)(2,1)S(1)}, u32[]{:S(2)}, u32[]{:S(2)}) collective-permute-start(bf16[512,128]{1,0:T(8,128)(2,1)S(1)} %get-tuple-element.93), channel_id=1, source_target_pairs={{0,64},{64,128},{128,192},{192,0},{1,65},{65,129},{129,193},{193,1... | collective-permute-start | bytes 393224 | tf_op jit(solution)/shard_map/ppermute | solution.py:393
  (28 other events, 204.3 us)

commit v2 on v1

--- a/solution.py
+++ b/solution.py
@@ -97,7 +97,7 @@
         gated = (att * inverse * gain_ref[:, cols]).astype(BF)
         gated_ref[cols, :] = gated.T
 
-    each(HEADS, step, 2)
+    each(HEADS, step, 4)
 
 
 def is_same():
@@ -223,11 +223,18 @@
     each(4, step)
 
 
-def pack_kernel(after1_ref, after2_ref, own_ref, r1_ref, r2_ref, r3_ref, out_ref, token_ref):
-    token_ref[...] = jnp.zeros(TOKEN[0], F32)
+def pack_kernel(
+    after1_ref, after2_ref, own_ref, r1_ref, r2_ref, r3_ref, out_ref, token_out, token, sems
+):
+    token[...] = jnp.zeros(TOKEN[0], F32)
     y = lax.axis_index("y")
+    copies = [pltpu.make_async_copy(token, token_out, sems.at[4])]
     for k, ref in enumerate((own_ref, r1_ref, r2_ref, r3_ref)):
-        out_ref[lax.rem(y + 4 - k, 4)] = ref[...]
+        copies.append(pltpu.make_async_copy(ref, out_ref.at[lax.rem(y + 4 - k, 4)], sems.at[k]))
+    for c in copies:
+        c.start()
+    for c in copies:
+        c.wait()
 
 
 def relay_rows_kernel(after1_ref, after2_ref, low_ref, high_ref, low_out, high_out, sems):
@@ -260,13 +267,13 @@
 
     n = len(values)
     anys = pl.BlockSpec(memory_space=pl.ANY)
-    vmem = pl.BlockSpec(memory_space=pltpu.VMEM)
     return pl.pallas_call(
         kernel,
         out_shape=tuple(jax.ShapeDtypeStruct(v.shape, v.dtype) for v in values),
-        in_specs=[anys] * n + [vmem] * len(deps),
+        in_specs=[anys] * (n + len(deps)),
         out_specs=(anys,) * n,
         input_output_aliases={i: i for i in range(n)},
+        compiler_params=pltpu.CompilerParams(vmem_limit_bytes=1 << 20),
         cost_estimate=pl.CostEstimate(flops=0, bytes_accessed=0, transcendentals=0),
     )(*values, *deps)
 
@@ -404,9 +411,15 @@
     state, state_token = call(state_kernel, [slices, TOKEN], 2, 1 << 27)(keys, values)
     states = lax.all_to_all(state, BLOCKS, 0, 0, tiled=True)
     others = [shift(out_weight, "y", 4, k) for k in (1, 2, 3)]
-    column, column_token = call(pack_kernel, [((4, 128, WIDTH), BF), TOKEN], 4, 1 << 20, 2)(
-        fwd, bwd, out_weight, *others
-    )
+    column, column_token = call(
+        pack_kernel,
+        [((4, 128, WIDTH), BF), TOKEN],
+        0,
+        1 << 20,
+        6,
+        [pltpu.VMEM(*TOKEN), pltpu.SemaphoreType.DMA((5,))],
+        True,
+    )(fwd, bwd, out_weight, *others)
     fwd, bwd = tie((fwd, bwd), (state_token, column_token))
     chunks = [own, fwd, bwd]
 

time: 126 us -> 119 us (0.944)
  local copies, waits for them, and re-layouts: 7.23 us -> 3.02 us
  Pallas kernels: 22.8 us -> 19.7 us
    unnamed x42 -> x16, local copies, waits for them, and re-layouts: 7.23 us -> 3.02 us
    pallas_call x2, Pallas kernels: 1.37 us -> 0.01 us  [tie(): pl.pallas_call(kernel, out_shape=tuple((jax.ShapeDtypeStruct(v.shape, v.d...]
  transfers between devices with their start and end apart: 31 -> 31, of which waited for: 12 -> 13; matrix products, arithmetic and copies ran while one was open for 0% -> 0% of each run, Pallas kernels for 13% -> 14%
where the time goes in v2:
time: 119 us
  starting transfers between devices  45 us (38%)
  blocking collectives  26.5 us (22%)
  waiting for transfers between devices  23.7 us (20%)
  Pallas kernels  19.7 us (17%)
  local copies, waits for them, and re-layouts  3.02 us (3%)
    ppermute x28, starting transfers between devices, shift(): return lax.ppermute(x, axis, pairs)  44.8 us
    ppermute x28, waiting for transfers between devices, shift(): return lax.ppermute(x, axis, pairs)  19.2 us
    all_to_all x1, blocking collectives, body(): states = lax.all_to_all(state, BLOCKS, 0, 0, tiled=True)  14.3 us
    all_to_all x1, blocking collectives, body(): prior = lax.all_to_all(priors, BLOCKS, 0, 0, tiled=True).reshape(STATE)  12.2 us
    pallas_call x1, Pallas kernels, body(): call(early_kernel, [(SQUARE, F32), wide, ((2, WIDTH, WIDTH), BF)], 3, 1 <...  5.63 us
    ppermute x3, waiting for transfers between devices, swap_cores(): return lax.ppermute(x, 'core', [(0, 1), (1, 0)])  4.59 us
    pallas_call x1, Pallas kernels, body(): call(post_kernel, [(SQUARE, BF), (SQUARE, F32), (SQUARE, F32), TOKEN], 5,...  4.38 us
    unnamed x16, local copies, waits for them, and re-layouts  3.02 us
  transfers between devices with their start and end apart: 31, of which 13 were waited for; matrix products, arithmetic and copies ran while one was open for 0% of the time, Pallas kernels for 14%

profile of v2, /device:TPU:6, one launch (start us, length us, event | category | flops | bytes accessed | tf_op | source)
XLA Modules:
  0.0 118.9 jit_solution(10503308595518269585)
XLA Ops:
  0.6 2.0 %collective-permute-start = (bf16[512,512]{1,0:T(8,128)(2,1)}, bf16[512,512]{1,0:T(8,128)(2,1)S(1)}, u32[]{:S(2)}, u32[]{:S(2)}) collective-permute-start(bf16[512,512]{1,0:T(8,128)(2,1)} %refs_0_.1), channel_id=1, source_target_pairs={{0,4},{4,8},{8,12},{12,16},{16,20},{20,24},{24,28},{28,0},{1,5},{5... | collective-permute-start | bytes 1572872 | tf_op jit(solution)/shard_map/ppermute | solution.py:400
  2.6 4.0 %collective-permute-start.1 = (bf16[512,512]{1,0:T(8,128)(2,1)}, bf16[512,512]{1,0:T(8,128)(2,1)S(1)}, u32[]{:S(2)}, u32[]{:S(2)}) collective-permute-start(bf16[512,512]{1,0:T(8,128)(2,1)} %refs_0_.1), channel_id=1, source_target_pairs={{0,28},{4,0},{8,4},{12,8},{16,12},{20,16},{24,20},{28,24},{1,29},{... | collective-permute-start | bytes 1572872 | tf_op jit(solution)/shard_map/ppermute | solution.py:400
  6.7 3.2 %collective-permute-start.3 = (bf16[128,512]{1,0:T(8,128)(2,1)}, bf16[128,512]{1,0:T(8,128)(2,1)S(1)}, u32[]{:S(2)}, u32[]{:S(2)}) collective-permute-start(bf16[128,512]{1,0:T(8,128)(2,1)} %own_ref.1), channel_id=1, source_target_pairs={{0,128},{64,192},{128,0},{192,64},{1,129},{65,193},{129,1},{193,65... | collective-permute-start | bytes 393224 | tf_op jit(solution)/shard_map/ppermute | solution.py:400
  10.5 2.6 %collective-permute-start.4 = (bf16[128,512]{1,0:T(8,128)(2,1)}, bf16[128,512]{1,0:T(8,128)(2,1)S(1)}, u32[]{:S(2)}, u32[]{:S(2)}) collective-permute-start(bf16[128,512]{1,0:T(8,128)(2,1)} %own_ref.1), channel_id=1, source_target_pairs={{0,192},{64,0},{128,64},{192,128},{1,193},{65,1},{129,65},{193,129... | collective-permute-start | bytes 393224 | tf_op jit(solution)/shard_map/ppermute | solution.py:400
  16.5 2.1 %collective-permute-done.after1_ref.refs_0_ = bf16[512,512]{1,0:T(8,128)(2,1)S(1)} collective-permute-done((bf16[512,512]{1,0:T(8,128)(2,1)}, bf16[512,512]{1,0:T(8,128)(2,1)S(1)}, u32[]{:S(2)}, u32[]{:S(2)}) %collective-permute-start) | collective-permute-done | bytes 524320 | tf_op jit(solution)/shard_map/ppermute | solution.py:400
  20.5 3.2 %collective-permute-start.6 = (bf16[512,512]{1,0:T(8,128)(2,1)S(1)}, bf16[512,512]{1,0:T(8,128)(2,1)S(1)}, u32[]{:S(2)}, u32[]{:S(2)}) collective-permute-start(bf16[512,512]{1,0:T(8,128)(2,1)S(1)} %get-tuple-element.56.refs_2_), channel_id=1, source_target_pairs={{0,28},{4,0},{8,4},{12,8},{16,12},{20,16},{24,20},{28,24},{1,29},{... | collective-permute-start | bytes 1572872 | tf_op jit(solution)/shard_map/ppermute | solution.py:400
  24.5 2.4 %collective-permute-start.9 = (bf16[4,128,512]{2,1,0:T(8,128)(2,1)S(1)}, bf16[4,128,512]{2,1,0:T(8,128)(2,1)S(1)}, u32[]{:S(2)}, u32[]{:S(2)}) collective-permute-start(bf16[4,128,512]{2,1,0:T(8,128)(2,1)S(1)} %get-tuple-element.60.own_ref), channel_id=1, source_target_pairs={{0,1},{1,2},{2,3},{3,0},{4,5},{5,6},{6,7},{7,4},{8,9},{9,10},{10,1... | collective-permute-start | bytes 1572872 | tf_op jit(solution)/shard_map/ppermute | solution.py:400
  26.9 14.3 %all_to_all.10.in_ref = bf16[32,16,128]{2,1,0:T(8,128)(2,1)S(1)} all-to-all(bf16[32,16,128]{2,1,0:T(8,128)(2,1)S(1)} %get-tuple-element.50), channel_id=1, replica_groups=mesh['y'=4,'core'=2,'tp'=8,'dp'=4] {'y','core','dp'}, dimensions={0} | all-to-all | bytes 262144 | tf_op jit(solution)/shard_map/all_to_all | solution.py:412
  41.5 3.2 %collective-permute-start.8 = (bf16[512,512]{1,0:T(8,128)(2,1)S(1)}, bf16[512,512]{1,0:T(8,128)(2,1)S(1)}, u32[]{:S(2)}, u32[]{:S(2)}) collective-permute-start(bf16[512,512]{1,0:T(8,128)(2,1)S(1)} %get-tuple-element.59.refs_4_), channel_id=1, source_target_pairs={{0,28},{4,0},{8,4},{12,8},{16,12},{20,16},{24,20},{28,24},{1,29},{... | collective-permute-start | bytes 1572872 | tf_op jit(solution)/shard_map/ppermute | solution.py:400
  44.7 3.2 %collective-permute-start.11 = (bf16[2,128,512]{2,1,0:T(8,128)(2,1)S(1)}, bf16[2,128,512]{2,1,0:T(8,128)(2,1)S(1)}, u32[]{:S(2)}, u32[]{:S(2)}) collective-permute-start(bf16[2,128,512]{2,1,0:T(8,128)(2,1)S(1)} %get-tuple-element.61), channel_id=1, source_target_pairs={{0,1},{1,2},{2,3},{3,0},{4,5},{5,6},{6,7},{7,4},{8,9},{9,10},{10,1... | collective-permute-start | bytes 786440 | tf_op jit(solution)/shard_map/ppermute | solution.py:400
  47.9 12.2 %all_to_all.11 = bf16[32,16,128]{2,1,0:T(8,128)(2,1)S(1)} all-to-all(bf16[32,16,128]{2,1,0:T(8,128)(2,1)S(1)} %get-tuple-element.51), channel_id=1, replica_groups=mesh['y'=4,'core'=2,'tp'=8,'dp'=4] {'y','core','dp'}, dimensions={0} | all-to-all | bytes 262144 | tf_op jit(solution)/shard_map/all_to_all | solution.py:428
  62.1 3.2 %collective-permute-start.14 = (bf16[256,512]{1,0:T(8,128)(2,1)S(1)}, bf16[256,512]{1,0:T(8,128)(2,1)S(1)}, u32[]{:S(2)}, u32[]{:S(2)}) collective-permute-start(bf16[256,512]{1,0:T(8,128)(2,1)S(1)} %get-tuple-element.64), channel_id=1, source_target_pairs={{0,28},{4,0},{8,4},{12,8},{16,12},{20,16},{24,20},{28,24},{1,29},{... | collective-permute-start | bytes 786440 | tf_op jit(solution)/shard_map/ppermute | solution.py:400
  66.1 5.6 %shard_map.109 = (f32[512,512]{1,0:T(8,128)S(1)}, bf16[8,512,512]{2,1,0:T(8,128)(2,1)S(1)}, bf16[2,512,512]{2,1,0:T(8,128)(2,1)S(1)}) custom-call(bf16[512,512]{1,0:T(8,128)(2,1)S(1)} %copy-done.7, bf16[512,512]{1,0:T(8,128)(2,1)S(1)} %get-tuple-element.55.refs_1_, bf16[512,512]{1,0:T(8,128)(2,1)S(1)} %get-tuple-element.56.refs_2_, ...), custom_call_target="tpu_custom_call" | custom-call | flops 8589934592 | bytes 4194304 | tf_op jit(solution)/shard_map/pallas_call | solution.py:452
  72.6 1.7 %shard_map.110 = (bf16[512,512]{1,0:T(8,128)(2,1)S(1)}, bf16[528,128]{1,0:T(8,128)(2,1)S(1)}, f32[8,128]{1,0:T(8,128)S(1)}) custom-call(bf16[256,512]{1,0:T(8,128)(2,1)S(1)} %collective-permute-done.13.low_ref, bf16[256,512]{1,0:T(8,128)(2,1)S(1)} %collective-permute-done.14.high_ref, bf16[2,512,512]{2,1,0:T(8,128)(2,1)S(1)} %get-tuple-element.66.weight_ref, ...), custom_call_target="tpu_custom_call" | custom-call | flops 1073741824 | bytes 4194304 | tf_op jit(solution)/shard_map/pallas_call | solution.py:463
  74.4 2.4 %collective-permute-done.16.got_ref = bf16[4,512,512]{2,1,0:T(8,128)(2,1)S(1)} collective-permute-done((bf16[4,512,512]{2,1,0:T(8,128)(2,1)S(1)}, bf16[4,512,512]{2,1,0:T(8,128)(2,1)S(1)}, u32[]{:S(2)}, u32[]{:S(2)}) %collective-permute-start.16) | collective-permute-done | bytes 2097184 | tf_op jit(solution)/shard_map/ppermute | solution.py:404
  77.7 1.7 %collective-permute-start.20 = (bf16[1024,128]{1,0:T(8,128)(2,1)S(1)}, bf16[1024,128]{1,0:T(8,128)(2,1)S(1)}, u32[]{:S(2)}, u32[]{:S(2)}) collective-permute-start(bf16[1024,128]{1,0:T(8,128)(2,1)S(1)} %get-tuple-element.81), channel_id=1, source_target_pairs={{0,1},{1,2},{2,3},{3,0},{4,5},{5,6},{6,7},{7,4},{8,9},{9,10},{10,1... | collective-permute-start | bytes 786440 | tf_op jit(solution)/shard_map/ppermute | solution.py:400
  79.8 2.9 %collective-permute-start.19 = (bf16[528,128]{1,0:T(8,128)(2,1)S(1)}, bf16[528,128]{1,0:T(8,128)(2,1)S(1)}, u32[]{:S(2)}, u32[]{:S(2)}) collective-permute-start(bf16[528,128]{1,0:T(8,128)(2,1)S(1)} %get-tuple-element.77.own_ref), channel_id=1, source_target_pairs={{0,1},{1,2},{2,3},{3,0},{4,5},{5,6},{6,7},{7,4},{8,9},{9,10},{10,1... | collective-permute-start | bytes 405512 | tf_op jit(solution)/shard_map/ppermute | solution.py:400
  83.5 6.3 %collective-permute-done.19.r3_ref = bf16[528,128]{1,0:T(8,128)(2,1)S(1)} collective-permute-done((bf16[528,128]{1,0:T(8,128)(2,1)S(1)}, bf16[528,128]{1,0:T(8,128)(2,1)S(1)}, u32[]{:S(2)}, u32[]{:S(2)}) %collective-permute-start.19) | collective-permute-done | bytes 135200 | tf_op jit(solution)/shard_map/ppermute | solution.py:400
  91.5 3.0 %collective-permute-done.17.r1_ref = bf16[528,128]{1,0:T(8,128)(2,1)S(1)} collective-permute-done((bf16[528,128]{1,0:T(8,128)(2,1)S(1)}, bf16[528,128]{1,0:T(8,128)(2,1)S(1)}, u32[]{:S(2)}, u32[]{:S(2)}) %collective-permute-start.17) | collective-permute-done | bytes 135200 | tf_op jit(solution)/shard_map/ppermute | solution.py:400
  95.2 1.7 %collective-permute-start.23 = (bf16[4,512,128]{2,1,0:T(8,128)(2,1)S(1)}, bf16[4,512,128]{2,1,0:T(8,128)(2,1)S(1)}, u32[]{:S(2)}, u32[]{:S(2)}) collective-permute-start(bf16[4,512,128]{2,1,0:T(8,128)(2,1)S(1)} %get-tuple-element.84), channel_id=1, source_target_pairs={{0,3},{1,0},{2,1},{3,2},{4,7},{5,4},{6,5},{7,6},{8,11},{9,8},{10,9... | collective-permute-start | bytes 1572872 | tf_op jit(solution)/shard_map/ppermute | solution.py:400
  99.0 2.0 %collective-permute-start.26 = (bf16[528,128]{1,0:T(8,128)(2,1)S(1)}, bf16[528,128]{1,0:T(8,128)(2,1)S(1)}, u32[]{:S(2)}, u32[]{:S(2)}) collective-permute-start(bf16[528,128]{1,0:T(8,128)(2,1)S(1)} %shard_map.117.own), channel_id=1, source_target_pairs={{0,128},{64,192},{128,0},{192,64},{1,129},{65,193},{129,1},{193,65... | collective-permute-start | bytes 405512 | tf_op jit(solution)/shard_map/ppermute | solution.py:400
  102.3 4.4 %shard_map.111 = (bf16[512,512]{1,0:T(8,128)(2,1)}, f32[512,512]{1,0:T(8,128)S(1)}, f32[512,512]{1,0:T(8,128)S(1)}, f32[8,128]{1,0:T(8,128)S(1)}) custom-call(bf16[512,512]{1,0:T(8,128)(2,1)S(1)} %copy-done.4, bf16[512,512]{1,0:T(8,128)(2,1)S(1)} %copy-done.1, bf16[512,512]{1,0:T(8,128)(2,1)S(1)} %copy-done.3, ...), custom_call_target="tpu_custom_call" | custom-call | flops 2147483648 | bytes 4194304 | tf_op jit(solution)/shard_map/pallas_call | solution.py:486
  110.2 2.0 %collective-permute-start.29 = (bf16[512,128]{1,0:T(8,128)(2,1)S(1)}, bf16[512,128]{1,0:T(8,128)(2,1)S(1)}, u32[]{:S(2)}, u32[]{:S(2)}) collective-permute-start(bf16[512,128]{1,0:T(8,128)(2,1)S(1)} %get-tuple-element.94), channel_id=1, source_target_pairs={{0,128},{64,192},{128,0},{192,64},{1,129},{65,193},{129,1},{193,65... | collective-permute-start | bytes 393224 | tf_op jit(solution)/shard_map/ppermute | solution.py:400
  115.1 2.0 %collective-permute-done.28.r1_ref = bf16[512,128]{1,0:T(8,128)(2,1)S(1)} collective-permute-done((bf16[512,128]{1,0:T(8,128)(2,1)S(1)}, bf16[512,128]{1,0:T(8,128)(2,1)S(1)}, u32[]{:S(2)}, u32[]{:S(2)}) %collective-permute-start.28) | collective-permute-done | bytes 131104 | tf_op jit(solution)/shard_map/ppermute | solution.py:400
  (75 shorter events, 26.5 us)
Async XLA Ops:
  0.6 18.1 %collective-permute-start = (bf16[512,512]{1,0:T(8,128)(2,1)}, bf16[512,512]{1,0:T(8,128)(2,1)S(1)}, u32[]{:S(2)}, u32[]{:S(2)}) collective-permute-start(bf16[512,512]{1,0:T(8,128)(2,1)} %refs_0_.1), channel_id=1, source_target_pairs={{0,4},{4,8},{8,12},{12,16},{16,20},{20,24},{24,28},{28,0},{1,5},{5... | collective-permute-start | bytes 1572872 | tf_op jit(solution)/shard_map/ppermute | solution.py:400
  2.6 16.1 %collective-permute-start.1 = (bf16[512,512]{1,0:T(8,128)(2,1)}, bf16[512,512]{1,0:T(8,128)(2,1)S(1)}, u32[]{:S(2)}, u32[]{:S(2)}) collective-permute-start(bf16[512,512]{1,0:T(8,128)(2,1)} %refs_0_.1), channel_id=1, source_target_pairs={{0,28},{4,0},{8,4},{12,8},{16,12},{20,16},{24,20},{28,24},{1,29},{... | collective-permute-start | bytes 1572872 | tf_op jit(solution)/shard_map/ppermute | solution.py:400
  6.7 9.4 %collective-permute-start.3 = (bf16[128,512]{1,0:T(8,128)(2,1)}, bf16[128,512]{1,0:T(8,128)(2,1)S(1)}, u32[]{:S(2)}, u32[]{:S(2)}) collective-permute-start(bf16[128,512]{1,0:T(8,128)(2,1)} %own_ref.1), channel_id=1, source_target_pairs={{0,128},{64,192},{128,0},{192,64},{1,129},{65,193},{129,1},{193,65... | collective-permute-start | bytes 393224 | tf_op jit(solution)/shard_map/ppermute | solution.py:400
  20.4 20.9 %collective-permute-start.5 = (bf16[512,512]{1,0:T(8,128)(2,1)S(1)}, bf16[512,512]{1,0:T(8,128)(2,1)S(1)}, u32[]{:S(2)}, u32[]{:S(2)}) collective-permute-start(bf16[512,512]{1,0:T(8,128)(2,1)S(1)} %get-tuple-element.55.refs_1_), channel_id=1, source_target_pairs={{0,4},{4,8},{8,12},{12,16},{16,20},{20,24},{24,28},{28,0},{1,5},{5... | collective-permute-start | bytes 1572872 | tf_op jit(solution)/shard_map/ppermute | solution.py:400
  20.5 20.8 %collective-permute-start.6 = (bf16[512,512]{1,0:T(8,128)(2,1)S(1)}, bf16[512,512]{1,0:T(8,128)(2,1)S(1)}, u32[]{:S(2)}, u32[]{:S(2)}) collective-permute-start(bf16[512,512]{1,0:T(8,128)(2,1)S(1)} %get-tuple-element.56.refs_2_), channel_id=1, source_target_pairs={{0,28},{4,0},{8,4},{12,8},{16,12},{20,16},{24,20},{28,24},{1,29},{... | collective-permute-start | bytes 1572872 | tf_op jit(solution)/shard_map/ppermute | solution.py:400
  23.7 17.6 %collective-permute-start.10 = (bf16[4,128,512]{2,1,0:T(8,128)(2,1)S(1)}, bf16[4,128,512]{2,1,0:T(8,128)(2,1)S(1)}, u32[]{:S(2)}, u32[]{:S(2)}) collective-permute-start(bf16[4,128,512]{2,1,0:T(8,128)(2,1)S(1)} %get-tuple-element.60.own_ref), channel_id=1, source_target_pairs={{0,3},{1,0},{2,1},{3,2},{4,7},{5,4},{6,5},{7,6},{8,11},{9,8},{10,9... | collective-permute-start | bytes 1572872 | tf_op jit(solution)/shard_map/ppermute | solution.py:400
  24.5 16.8 %collective-permute-start.9 = (bf16[4,128,512]{2,1,0:T(8,128)(2,1)S(1)}, bf16[4,128,512]{2,1,0:T(8,128)(2,1)S(1)}, u32[]{:S(2)}, u32[]{:S(2)}) collective-permute-start(bf16[4,128,512]{2,1,0:T(8,128)(2,1)S(1)} %get-tuple-element.60.own_ref), channel_id=1, source_target_pairs={{0,1},{1,2},{2,3},{3,0},{4,5},{5,6},{6,7},{7,4},{8,9},{9,10},{10,1... | collective-permute-start | bytes 1572872 | tf_op jit(solution)/shard_map/ppermute | solution.py:400
  41.4 20.3 %collective-permute-start.7 = (bf16[512,512]{1,0:T(8,128)(2,1)S(1)}, bf16[512,512]{1,0:T(8,128)(2,1)S(1)}, u32[]{:S(2)}, u32[]{:S(2)}) collective-permute-start(bf16[512,512]{1,0:T(8,128)(2,1)S(1)} %get-tuple-element.58.refs_3_), channel_id=1, source_target_pairs={{0,4},{4,8},{8,12},{12,16},{16,20},{20,24},{24,28},{28,0},{1,5},{5... | collective-permute-start | bytes 1572872 | tf_op jit(solution)/shard_map/ppermute | solution.py:400
  41.5 20.2 %collective-permute-start.8 = (bf16[512,512]{1,0:T(8,128)(2,1)S(1)}, bf16[512,512]{1,0:T(8,128)(2,1)S(1)}, u32[]{:S(2)}, u32[]{:S(2)}) collective-permute-start(bf16[512,512]{1,0:T(8,128)(2,1)S(1)} %get-tuple-element.59.refs_4_), channel_id=1, source_target_pairs={{0,28},{4,0},{8,4},{12,8},{16,12},{20,16},{24,20},{28,24},{1,29},{... | collective-permute-start | bytes 1572872 | tf_op jit(solution)/shard_map/ppermute | solution.py:400
  44.7 17.0 %collective-permute-start.11 = (bf16[2,128,512]{2,1,0:T(8,128)(2,1)S(1)}, bf16[2,128,512]{2,1,0:T(8,128)(2,1)S(1)}, u32[]{:S(2)}, u32[]{:S(2)}) collective-permute-start(bf16[2,128,512]{2,1,0:T(8,128)(2,1)S(1)} %get-tuple-element.61), channel_id=1, source_target_pairs={{0,1},{1,2},{2,3},{3,0},{4,5},{5,6},{6,7},{7,4},{8,9},{9,10},{10,1... | collective-permute-start | bytes 786440 | tf_op jit(solution)/shard_map/ppermute | solution.py:400
  47.9 13.8 %collective-permute-start.12 = (bf16[2,128,512]{2,1,0:T(8,128)(2,1)S(1)}, bf16[2,128,512]{2,1,0:T(8,128)(2,1)S(1)}, u32[]{:S(2)}, u32[]{:S(2)}) collective-permute-start(bf16[2,128,512]{2,1,0:T(8,128)(2,1)S(1)} %get-tuple-element.62), channel_id=1, source_target_pairs={{0,3},{1,0},{2,1},{3,2},{4,7},{5,4},{6,5},{7,6},{8,11},{9,8},{10,9... | collective-permute-start | bytes 786440 | tf_op jit(solution)/shard_map/ppermute | solution.py:400
  62.0 9.9 %collective-permute-start.13 = (bf16[256,512]{1,0:T(8,128)(2,1)S(1)}, bf16[256,512]{1,0:T(8,128)(2,1)S(1)}, u32[]{:S(2)}, u32[]{:S(2)}) collective-permute-start(bf16[256,512]{1,0:T(8,128)(2,1)S(1)} %get-tuple-element.63), channel_id=1, source_target_pairs={{0,4},{4,8},{8,12},{12,16},{16,20},{20,24},{24,28},{28,0},{1,5},{5... | collective-permute-start | bytes 786440 | tf_op jit(solution)/shard_map/ppermute | solution.py:400
  62.1 9.8 %collective-permute-start.14 = (bf16[256,512]{1,0:T(8,128)(2,1)S(1)}, bf16[256,512]{1,0:T(8,128)(2,1)S(1)}, u32[]{:S(2)}, u32[]{:S(2)}) collective-permute-start(bf16[256,512]{1,0:T(8,128)(2,1)S(1)} %get-tuple-element.64), channel_id=1, source_target_pairs={{0,28},{4,0},{8,4},{12,8},{16,12},{20,16},{24,20},{28,24},{1,29},{... | collective-permute-start | bytes 786440 | tf_op jit(solution)/shard_map/ppermute | solution.py:400
  77.7 17.0 %collective-permute-start.20 = (bf16[1024,128]{1,0:T(8,128)(2,1)S(1)}, bf16[1024,128]{1,0:T(8,128)(2,1)S(1)}, u32[]{:S(2)}, u32[]{:S(2)}) collective-permute-start(bf16[1024,128]{1,0:T(8,128)(2,1)S(1)} %get-tuple-element.81), channel_id=1, source_target_pairs={{0,1},{1,2},{2,3},{3,0},{4,5},{5,6},{6,7},{7,4},{8,9},{9,10},{10,1... | collective-permute-start | bytes 786440 | tf_op jit(solution)/shard_map/ppermute | solution.py:400
  79.4 15.2 %collective-permute-start.21 = (bf16[1024,128]{1,0:T(8,128)(2,1)S(1)}, bf16[1024,128]{1,0:T(8,128)(2,1)S(1)}, u32[]{:S(2)}, u32[]{:S(2)}) collective-permute-start(bf16[1024,128]{1,0:T(8,128)(2,1)S(1)} %get-tuple-element.82), channel_id=1, source_target_pairs={{0,3},{1,0},{2,1},{3,2},{4,7},{5,4},{6,5},{7,6},{8,11},{9,8},{10,9... | collective-permute-start | bytes 786440 | tf_op jit(solution)/shard_map/ppermute | solution.py:400
  79.8 10.0 %collective-permute-start.19 = (bf16[528,128]{1,0:T(8,128)(2,1)S(1)}, bf16[528,128]{1,0:T(8,128)(2,1)S(1)}, u32[]{:S(2)}, u32[]{:S(2)}) collective-permute-start(bf16[528,128]{1,0:T(8,128)(2,1)S(1)} %get-tuple-element.77.own_ref), channel_id=1, source_target_pairs={{0,1},{1,2},{2,3},{3,0},{4,5},{5,6},{6,7},{7,4},{8,9},{9,10},{10,1... | collective-permute-start | bytes 405512 | tf_op jit(solution)/shard_map/ppermute | solution.py:400
  82.7 8.8 %collective-permute-start.18 = (bf16[528,128]{1,0:T(8,128)(2,1)S(1)}, bf16[528,128]{1,0:T(8,128)(2,1)S(1)}, u32[]{:S(2)}, u32[]{:S(2)}) collective-permute-start(bf16[528,128]{1,0:T(8,128)(2,1)S(1)} %get-tuple-element.77.own_ref), channel_id=1, source_target_pairs={{0,2},{1,3},{2,0},{3,1},{4,6},{5,7},{6,4},{7,5},{8,10},{9,11},{10,... | collective-permute-start | bytes 405512 | tf_op jit(solution)/shard_map/ppermute | solution.py:400
  82.7 11.8 %collective-permute-start.17 = (bf16[528,128]{1,0:T(8,128)(2,1)S(1)}, bf16[528,128]{1,0:T(8,128)(2,1)S(1)}, u32[]{:S(2)}, u32[]{:S(2)}) collective-permute-start(bf16[528,128]{1,0:T(8,128)(2,1)S(1)} %get-tuple-element.77.own_ref), channel_id=1, source_target_pairs={{0,3},{1,0},{2,1},{3,2},{4,7},{5,4},{6,5},{7,6},{8,11},{9,8},{10,9... | collective-permute-start | bytes 405512 | tf_op jit(solution)/shard_map/ppermute | solution.py:400
  94.8 12.9 %collective-permute-start.22 = (bf16[4,512,128]{2,1,0:T(8,128)(2,1)S(1)}, bf16[4,512,128]{2,1,0:T(8,128)(2,1)S(1)}, u32[]{:S(2)}, u32[]{:S(2)}) collective-permute-start(bf16[4,512,128]{2,1,0:T(8,128)(2,1)S(1)} %get-tuple-element.83), channel_id=1, source_target_pairs={{0,1},{1,2},{2,3},{3,0},{4,5},{5,6},{6,7},{7,4},{8,9},{9,10},{10,1... | collective-permute-start | bytes 1572872 | tf_op jit(solution)/shard_map/ppermute | solution.py:400
  95.2 14.1 %collective-permute-start.23 = (bf16[4,512,128]{2,1,0:T(8,128)(2,1)S(1)}, bf16[4,512,128]{2,1,0:T(8,128)(2,1)S(1)}, u32[]{:S(2)}, u32[]{:S(2)}) collective-permute-start(bf16[4,512,128]{2,1,0:T(8,128)(2,1)S(1)} %get-tuple-element.84), channel_id=1, source_target_pairs={{0,3},{1,0},{2,1},{3,2},{4,7},{5,4},{6,5},{7,6},{8,11},{9,8},{10,9... | collective-permute-start | bytes 1572872 | tf_op jit(solution)/shard_map/ppermute | solution.py:400
  98.3 13.8 %collective-permute-start.27 = (bf16[528,128]{1,0:T(8,128)(2,1)S(1)}, bf16[528,128]{1,0:T(8,128)(2,1)S(1)}, u32[]{:S(2)}, u32[]{:S(2)}) collective-permute-start(bf16[528,128]{1,0:T(8,128)(2,1)S(1)} %shard_map.117.own), channel_id=1, source_target_pairs={{0,64},{64,128},{128,192},{192,0},{1,65},{65,129},{129,193},{193,1... | collective-permute-start | bytes 405512 | tf_op jit(solution)/shard_map/ppermute | solution.py:400
  99.0 14.5 %collective-permute-start.26 = (bf16[528,128]{1,0:T(8,128)(2,1)S(1)}, bf16[528,128]{1,0:T(8,128)(2,1)S(1)}, u32[]{:S(2)}, u32[]{:S(2)}) collective-permute-start(bf16[528,128]{1,0:T(8,128)(2,1)S(1)} %shard_map.117.own), channel_id=1, source_target_pairs={{0,128},{64,192},{128,0},{192,64},{1,129},{65,193},{129,1},{193,65... | collective-permute-start | bytes 405512 | tf_op jit(solution)/shard_map/ppermute | solution.py:400
  101.0 12.5 %collective-permute-start.25 = (bf16[528,128]{1,0:T(8,128)(2,1)S(1)}, bf16[528,128]{1,0:T(8,128)(2,1)S(1)}, u32[]{:S(2)}, u32[]{:S(2)}) collective-permute-start(bf16[528,128]{1,0:T(8,128)(2,1)S(1)} %shard_map.117.own), channel_id=1, source_target_pairs={{0,192},{64,0},{128,64},{192,128},{1,193},{65,1},{129,65},{193,129... | collective-permute-start | bytes 405512 | tf_op jit(solution)/shard_map/ppermute | solution.py:400
  109.5 7.7 %collective-permute-start.28 = (bf16[512,128]{1,0:T(8,128)(2,1)S(1)}, bf16[512,128]{1,0:T(8,128)(2,1)S(1)}, u32[]{:S(2)}, u32[]{:S(2)}) collective-permute-start(bf16[512,128]{1,0:T(8,128)(2,1)S(1)} %get-tuple-element.93), channel_id=1, source_target_pairs={{0,64},{64,128},{128,192},{192,0},{1,65},{65,129},{129,193},{193,1... | collective-permute-start | bytes 393224 | tf_op jit(solution)/shard_map/ppermute | solution.py:400
  (15 other events, 201.8 us)

commit v3 on v2

--- a/solution.py
+++ b/solution.py
@@ -480,8 +480,10 @@
     total, after = call(row_back_kernel, [(STATE_GAIN, BF), (STATE, F32)], 4, 1 << 22)(
         send, *[shift(send, "dp", 4, -k) for k in (1, 2, 3)]
     )
+    other = swap_cores(total)
+    (both,) = call(pair_back_kernel, [(STATE_GAIN, BF)], 2, 1 << 22)(total, other)
     up, down = call(relay_kernel, [quarter, quarter], 4, 1 << 20, 1)(
-        total, up, down, shift(low, "dp", 4, 1), shift(high, "dp", 4, -1)
+        both, up, down, shift(low, "dp", 4, 1), shift(high, "dp", 4, -1)
     )
     query_grad, key_part, value_part, token = call(
         post_kernel, [(SQUARE, BF), (SQUARE, F32), (SQUARE, F32), TOKEN], 5, 1 << 31
@@ -498,8 +500,6 @@
     (weight_grad,) = call(sum_kernel, [((128, WIDTH), F32)], 4, 1 << 20)(
         part, shift(up, "y", 4, 1), shift(away, "y", 4, 2), shift(down, "y", 4, -1)
     )
-    other = swap_cores(total)
-    (both,) = call(pair_back_kernel, [(STATE_GAIN, BF)], 2, 1 << 22)(total, other)
     upper = [shift(both, "y", 4, -k) for k in (1, 2, 3)]
     key_grad, value_grad, gain_sum = call(
         final_kernel, [(SQUARE, BF), (SQUARE, BF), ((HEADS, HEAD_DIM), F32)], 10, 1 << 28, 1

time: 119 us -> 117 us (0.983)
  waiting for transfers between devices: 23.7 us -> 21.8 us
    ppermute x3, waiting for transfers between devices: 4.59 us -> 2.17 us  [swap_cores(): return lax.ppermute(x, 'core', [(0, 1), (1, 0)])]
  transfers between devices with their start and end apart: 31 -> 31, of which waited for: 13 -> 13; matrix products, arithmetic and copies ran while one was open for 0% -> 0% of each run, Pallas kernels for 14% -> 15%
where the time goes in v3:
time: 117 us
  starting transfers between devices  45.3 us (39%)
  blocking collectives  26.5 us (23%)
  waiting for transfers between devices  21.8 us (19%)
  Pallas kernels  19.7 us (17%)
  local copies, waits for them, and re-layouts  3.02 us (3%)
    ppermute x28, starting transfers between devices, shift(): return lax.ppermute(x, axis, pairs)  45 us
    ppermute x28, waiting for transfers between devices, shift(): return lax.ppermute(x, axis, pairs)  19.6 us
    all_to_all x1, blocking collectives, body(): states = lax.all_to_all(state, BLOCKS, 0, 0, tiled=True)  14.3 us
    all_to_all x1, blocking collectives, body(): prior = lax.all_to_all(priors, BLOCKS, 0, 0, tiled=True).reshape(STATE)  12.2 us
    pallas_call x1, Pallas kernels, body(): call(early_kernel, [(SQUARE, F32), wide, ((2, WIDTH, WIDTH), BF)], 3, 1 <...  5.63 us
    pallas_call x1, Pallas kernels, body(): call(post_kernel, [(SQUARE, BF), (SQUARE, F32), (SQUARE, F32), TOKEN], 5,...  4.37 us
    unnamed x16, local copies, waits for them, and re-layouts  3.02 us
  transfers between devices with their start and end apart: 31, of which 13 were waited for; matrix products, arithmetic and copies ran while one was open for 0% of the time, Pallas kernels for 15%

profile of v3, /device:TPU:6, one launch (start us, length us, event | category | flops | bytes accessed | tf_op | source)
XLA Modules:
  0.0 117.2 jit_solution(10481505890098378899)
XLA Ops:
  0.6 2.0 %collective-permute-start = (bf16[512,512]{1,0:T(8,128)(2,1)}, bf16[512,512]{1,0:T(8,128)(2,1)S(1)}, u32[]{:S(2)}, u32[]{:S(2)}) collective-permute-start(bf16[512,512]{1,0:T(8,128)(2,1)} %refs_0_.1), channel_id=1, source_target_pairs={{0,4},{4,8},{8,12},{12,16},{16,20},{20,24},{24,28},{28,0},{1,5},{5... | collective-permute-start | bytes 1572872 | tf_op jit(solution)/shard_map/ppermute | solution.py:400
  2.6 4.0 %collective-permute-start.1 = (bf16[512,512]{1,0:T(8,128)(2,1)}, bf16[512,512]{1,0:T(8,128)(2,1)S(1)}, u32[]{:S(2)}, u32[]{:S(2)}) collective-permute-start(bf16[512,512]{1,0:T(8,128)(2,1)} %refs_0_.1), channel_id=1, source_target_pairs={{0,28},{4,0},{8,4},{12,8},{16,12},{20,16},{24,20},{28,24},{1,29},{... | collective-permute-start | bytes 1572872 | tf_op jit(solution)/shard_map/ppermute | solution.py:400
  6.7 3.2 %collective-permute-start.3 = (bf16[128,512]{1,0:T(8,128)(2,1)}, bf16[128,512]{1,0:T(8,128)(2,1)S(1)}, u32[]{:S(2)}, u32[]{:S(2)}) collective-permute-start(bf16[128,512]{1,0:T(8,128)(2,1)} %own_ref.1), channel_id=1, source_target_pairs={{0,128},{64,192},{128,0},{192,64},{1,129},{65,193},{129,1},{193,65... | collective-permute-start | bytes 393224 | tf_op jit(solution)/shard_map/ppermute | solution.py:400
  10.5 2.6 %collective-permute-start.4 = (bf16[128,512]{1,0:T(8,128)(2,1)}, bf16[128,512]{1,0:T(8,128)(2,1)S(1)}, u32[]{:S(2)}, u32[]{:S(2)}) collective-permute-start(bf16[128,512]{1,0:T(8,128)(2,1)} %own_ref.1), channel_id=1, source_target_pairs={{0,192},{64,0},{128,64},{192,128},{1,193},{65,1},{129,65},{193,129... | collective-permute-start | bytes 393224 | tf_op jit(solution)/shard_map/ppermute | solution.py:400
  16.5 2.1 %collective-permute-done.after1_ref.refs_0_ = bf16[512,512]{1,0:T(8,128)(2,1)S(1)} collective-permute-done((bf16[512,512]{1,0:T(8,128)(2,1)}, bf16[512,512]{1,0:T(8,128)(2,1)S(1)}, u32[]{:S(2)}, u32[]{:S(2)}) %collective-permute-start) | collective-permute-done | bytes 524320 | tf_op jit(solution)/shard_map/ppermute | solution.py:400
  20.5 3.2 %collective-permute-start.6 = (bf16[512,512]{1,0:T(8,128)(2,1)S(1)}, bf16[512,512]{1,0:T(8,128)(2,1)S(1)}, u32[]{:S(2)}, u32[]{:S(2)}) collective-permute-start(bf16[512,512]{1,0:T(8,128)(2,1)S(1)} %get-tuple-element.56.refs_2_), channel_id=1, source_target_pairs={{0,28},{4,0},{8,4},{12,8},{16,12},{20,16},{24,20},{28,24},{1,29},{... | collective-permute-start | bytes 1572872 | tf_op jit(solution)/shard_map/ppermute | solution.py:400
  24.5 2.4 %collective-permute-start.9 = (bf16[4,128,512]{2,1,0:T(8,128)(2,1)S(1)}, bf16[4,128,512]{2,1,0:T(8,128)(2,1)S(1)}, u32[]{:S(2)}, u32[]{:S(2)}) collective-permute-start(bf16[4,128,512]{2,1,0:T(8,128)(2,1)S(1)} %get-tuple-element.60.own_ref), channel_id=1, source_target_pairs={{0,1},{1,2},{2,3},{3,0},{4,5},{5,6},{6,7},{7,4},{8,9},{9,10},{10,1... | collective-permute-start | bytes 1572872 | tf_op jit(solution)/shard_map/ppermute | solution.py:400
  26.9 14.3 %all_to_all.10.in_ref = bf16[32,16,128]{2,1,0:T(8,128)(2,1)S(1)} all-to-all(bf16[32,16,128]{2,1,0:T(8,128)(2,1)S(1)} %get-tuple-element.50), channel_id=1, replica_groups=mesh['y'=4,'core'=2,'tp'=8,'dp'=4] {'y','core','dp'}, dimensions={0} | all-to-all | bytes 262144 | tf_op jit(solution)/shard_map/all_to_all | solution.py:412
  41.5 3.2 %collective-permute-start.8 = (bf16[512,512]{1,0:T(8,128)(2,1)S(1)}, bf16[512,512]{1,0:T(8,128)(2,1)S(1)}, u32[]{:S(2)}, u32[]{:S(2)}) collective-permute-start(bf16[512,512]{1,0:T(8,128)(2,1)S(1)} %get-tuple-element.59.refs_4_), channel_id=1, source_target_pairs={{0,28},{4,0},{8,4},{12,8},{16,12},{20,16},{24,20},{28,24},{1,29},{... | collective-permute-start | bytes 1572872 | tf_op jit(solution)/shard_map/ppermute | solution.py:400
  44.7 3.2 %collective-permute-start.11 = (bf16[2,128,512]{2,1,0:T(8,128)(2,1)S(1)}, bf16[2,128,512]{2,1,0:T(8,128)(2,1)S(1)}, u32[]{:S(2)}, u32[]{:S(2)}) collective-permute-start(bf16[2,128,512]{2,1,0:T(8,128)(2,1)S(1)} %get-tuple-element.61), channel_id=1, source_target_pairs={{0,1},{1,2},{2,3},{3,0},{4,5},{5,6},{6,7},{7,4},{8,9},{9,10},{10,1... | collective-permute-start | bytes 786440 | tf_op jit(solution)/shard_map/ppermute | solution.py:400
  47.9 12.2 %all_to_all.11 = bf16[32,16,128]{2,1,0:T(8,128)(2,1)S(1)} all-to-all(bf16[32,16,128]{2,1,0:T(8,128)(2,1)S(1)} %get-tuple-element.51), channel_id=1, replica_groups=mesh['y'=4,'core'=2,'tp'=8,'dp'=4] {'y','core','dp'}, dimensions={0} | all-to-all | bytes 262144 | tf_op jit(solution)/shard_map/all_to_all | solution.py:428
  62.1 3.2 %collective-permute-start.14 = (bf16[256,512]{1,0:T(8,128)(2,1)S(1)}, bf16[256,512]{1,0:T(8,128)(2,1)S(1)}, u32[]{:S(2)}, u32[]{:S(2)}) collective-permute-start(bf16[256,512]{1,0:T(8,128)(2,1)S(1)} %get-tuple-element.64), channel_id=1, source_target_pairs={{0,28},{4,0},{8,4},{12,8},{16,12},{20,16},{24,20},{28,24},{1,29},{... | collective-permute-start | bytes 786440 | tf_op jit(solution)/shard_map/ppermute | solution.py:400
  66.1 5.6 %shard_map.109 = (f32[512,512]{1,0:T(8,128)S(1)}, bf16[8,512,512]{2,1,0:T(8,128)(2,1)S(1)}, bf16[2,512,512]{2,1,0:T(8,128)(2,1)S(1)}) custom-call(bf16[512,512]{1,0:T(8,128)(2,1)S(1)} %copy-done.7, bf16[512,512]{1,0:T(8,128)(2,1)S(1)} %get-tuple-element.55.refs_1_, bf16[512,512]{1,0:T(8,128)(2,1)S(1)} %get-tuple-element.56.refs_2_, ...), custom_call_target="tpu_custom_call" | custom-call | flops 8589934592 | bytes 4194304 | tf_op jit(solution)/shard_map/pallas_call | solution.py:452
  72.6 1.7 %shard_map.110 = (bf16[512,512]{1,0:T(8,128)(2,1)S(1)}, bf16[528,128]{1,0:T(8,128)(2,1)S(1)}, f32[8,128]{1,0:T(8,128)S(1)}) custom-call(bf16[256,512]{1,0:T(8,128)(2,1)S(1)} %collective-permute-done.13.low_ref, bf16[256,512]{1,0:T(8,128)(2,1)S(1)} %collective-permute-done.14.high_ref, bf16[2,512,512]{2,1,0:T(8,128)(2,1)S(1)} %get-tuple-element.66.weight_ref, ...), custom_call_target="tpu_custom_call" | custom-call | flops 1073741824 | bytes 4194304 | tf_op jit(solution)/shard_map/pallas_call | solution.py:463
  74.4 1.9 %collective-permute-start.19 = (bf16[528,128]{1,0:T(8,128)(2,1)S(1)}, bf16[528,128]{1,0:T(8,128)(2,1)S(1)}, u32[]{:S(2)}, u32[]{:S(2)}) collective-permute-start(bf16[528,128]{1,0:T(8,128)(2,1)S(1)} %get-tuple-element.77.own_ref), channel_id=1, source_target_pairs={{0,1},{1,2},{2,3},{3,0},{4,5},{5,6},{6,7},{7,4},{8,9},{9,10},{10,1... | collective-permute-start | bytes 405512 | tf_op jit(solution)/shard_map/ppermute | solution.py:400
  78.5 2.6 %collective-permute-start.21 = (bf16[1024,128]{1,0:T(8,128)(2,1)S(1)}, bf16[1024,128]{1,0:T(8,128)(2,1)S(1)}, u32[]{:S(2)}, u32[]{:S(2)}) collective-permute-start(bf16[1024,128]{1,0:T(8,128)(2,1)S(1)} %get-tuple-element.81), channel_id=1, source_target_pairs={{0,1},{1,2},{2,3},{3,0},{4,5},{5,6},{6,7},{7,4},{8,9},{9,10},{10,1... | collective-permute-start | bytes 786440 | tf_op jit(solution)/shard_map/ppermute | solution.py:400
  81.2 3.0 %collective-permute-done.18.r2_ref = bf16[528,128]{1,0:T(8,128)(2,1)S(1)} collective-permute-done((bf16[528,128]{1,0:T(8,128)(2,1)S(1)}, bf16[528,128]{1,0:T(8,128)(2,1)S(1)}, u32[]{:S(2)}, u32[]{:S(2)}) %collective-permute-start.18) | collective-permute-done | bytes 135200 | tf_op jit(solution)/shard_map/ppermute | solution.py:400
  84.2 2.1 %collective-permute-done.17.r1_ref = bf16[528,128]{1,0:T(8,128)(2,1)S(1)} collective-permute-done((bf16[528,128]{1,0:T(8,128)(2,1)S(1)}, bf16[528,128]{1,0:T(8,128)(2,1)S(1)}, u32[]{:S(2)}, u32[]{:S(2)}) %collective-permute-start.17) | collective-permute-done | bytes 135200 | tf_op jit(solution)/shard_map/ppermute | solution.py:400
  89.0 2.8 %collective-permute-done.22.high_ref = bf16[1024,128]{1,0:T(8,128)(2,1)S(1)} collective-permute-done((bf16[1024,128]{1,0:T(8,128)(2,1)S(1)}, bf16[1024,128]{1,0:T(8,128)(2,1)S(1)}, u32[]{:S(2)}, u32[]{:S(2)}) %collective-permute-start.22) | collective-permute-done | bytes 262176 | tf_op jit(solution)/shard_map/ppermute | solution.py:400
  94.9 2.0 %collective-permute-start.26 = (bf16[528,128]{1,0:T(8,128)(2,1)S(1)}, bf16[528,128]{1,0:T(8,128)(2,1)S(1)}, u32[]{:S(2)}, u32[]{:S(2)}) collective-permute-start(bf16[528,128]{1,0:T(8,128)(2,1)S(1)} %shard_map.115.after_ref.own), channel_id=1, source_target_pairs={{0,128},{64,192},{128,0},{192,64},{1,129},{65,193},{129,1},{193,65... | collective-permute-start | bytes 405512 | tf_op jit(solution)/shard_map/ppermute | solution.py:400
  98.2 4.4 %shard_map.111 = (bf16[512,512]{1,0:T(8,128)(2,1)}, f32[512,512]{1,0:T(8,128)S(1)}, f32[512,512]{1,0:T(8,128)S(1)}, f32[8,128]{1,0:T(8,128)S(1)}) custom-call(bf16[512,512]{1,0:T(8,128)(2,1)S(1)} %copy-done.4, bf16[512,512]{1,0:T(8,128)(2,1)S(1)} %copy-done.1, bf16[512,512]{1,0:T(8,128)(2,1)S(1)} %copy-done.3, ...), custom_call_target="tpu_custom_call" | custom-call | flops 2147483648 | bytes 4194304 | tf_op jit(solution)/shard_map/pallas_call | solution.py:488
  102.6 3.5 %collective-permute-done.23.a_ref = bf16[4,512,128]{2,1,0:T(8,128)(2,1)S(1)} collective-permute-done((bf16[4,512,128]{2,1,0:T(8,128)(2,1)S(1)}, bf16[4,512,128]{2,1,0:T(8,128)(2,1)S(1)}, u32[]{:S(2)}, u32[]{:S(2)}) %collective-permute-start.23) | collective-permute-done | bytes 524320 | tf_op jit(solution)/shard_map/ppermute | solution.py:400
  108.3 2.0 %collective-permute-start.29 = (bf16[512,128]{1,0:T(8,128)(2,1)S(1)}, bf16[512,128]{1,0:T(8,128)(2,1)S(1)}, u32[]{:S(2)}, u32[]{:S(2)}) collective-permute-start(bf16[512,128]{1,0:T(8,128)(2,1)S(1)} %get-tuple-element.94), channel_id=1, source_target_pairs={{0,128},{64,192},{128,0},{192,64},{1,129},{65,193},{129,1},{193,65... | collective-permute-start | bytes 393224 | tf_op jit(solution)/shard_map/ppermute | solution.py:400
  113.3 2.5 %collective-permute-done.28.r1_ref = bf16[512,128]{1,0:T(8,128)(2,1)S(1)} collective-permute-done((bf16[512,128]{1,0:T(8,128)(2,1)S(1)}, bf16[512,128]{1,0:T(8,128)(2,1)S(1)}, u32[]{:S(2)}, u32[]{:S(2)}) %collective-permute-start.28) | collective-permute-done | bytes 131104 | tf_op jit(solution)/shard_map/ppermute | solution.py:400
  (75 shorter events, 26.6 us)
Async XLA Ops:
  0.6 18.1 %collective-permute-start = (bf16[512,512]{1,0:T(8,128)(2,1)}, bf16[512,512]{1,0:T(8,128)(2,1)S(1)}, u32[]{:S(2)}, u32[]{:S(2)}) collective-permute-start(bf16[512,512]{1,0:T(8,128)(2,1)} %refs_0_.1), channel_id=1, source_target_pairs={{0,4},{4,8},{8,12},{12,16},{16,20},{20,24},{24,28},{28,0},{1,5},{5... | collective-permute-start | bytes 1572872 | tf_op jit(solution)/shard_map/ppermute | solution.py:400
  2.6 16.1 %collective-permute-start.1 = (bf16[512,512]{1,0:T(8,128)(2,1)}, bf16[512,512]{1,0:T(8,128)(2,1)S(1)}, u32[]{:S(2)}, u32[]{:S(2)}) collective-permute-start(bf16[512,512]{1,0:T(8,128)(2,1)} %refs_0_.1), channel_id=1, source_target_pairs={{0,28},{4,0},{8,4},{12,8},{16,12},{20,16},{24,20},{28,24},{1,29},{... | collective-permute-start | bytes 1572872 | tf_op jit(solution)/shard_map/ppermute | solution.py:400
  6.7 9.4 %collective-permute-start.3 = (bf16[128,512]{1,0:T(8,128)(2,1)}, bf16[128,512]{1,0:T(8,128)(2,1)S(1)}, u32[]{:S(2)}, u32[]{:S(2)}) collective-permute-start(bf16[128,512]{1,0:T(8,128)(2,1)} %own_ref.1), channel_id=1, source_target_pairs={{0,128},{64,192},{128,0},{192,64},{1,129},{65,193},{129,1},{193,65... | collective-permute-start | bytes 393224 | tf_op jit(solution)/shard_map/ppermute | solution.py:400
  20.4 20.9 %collective-permute-start.5 = (bf16[512,512]{1,0:T(8,128)(2,1)S(1)}, bf16[512,512]{1,0:T(8,128)(2,1)S(1)}, u32[]{:S(2)}, u32[]{:S(2)}) collective-permute-start(bf16[512,512]{1,0:T(8,128)(2,1)S(1)} %get-tuple-element.55.refs_1_), channel_id=1, source_target_pairs={{0,4},{4,8},{8,12},{12,16},{16,20},{20,24},{24,28},{28,0},{1,5},{5... | collective-permute-start | bytes 1572872 | tf_op jit(solution)/shard_map/ppermute | solution.py:400
  20.5 20.8 %collective-permute-start.6 = (bf16[512,512]{1,0:T(8,128)(2,1)S(1)}, bf16[512,512]{1,0:T(8,128)(2,1)S(1)}, u32[]{:S(2)}, u32[]{:S(2)}) collective-permute-start(bf16[512,512]{1,0:T(8,128)(2,1)S(1)} %get-tuple-element.56.refs_2_), channel_id=1, source_target_pairs={{0,28},{4,0},{8,4},{12,8},{16,12},{20,16},{24,20},{28,24},{1,29},{... | collective-permute-start | bytes 1572872 | tf_op jit(solution)/shard_map/ppermute | solution.py:400
  23.7 17.6 %collective-permute-start.10 = (bf16[4,128,512]{2,1,0:T(8,128)(2,1)S(1)}, bf16[4,128,512]{2,1,0:T(8,128)(2,1)S(1)}, u32[]{:S(2)}, u32[]{:S(2)}) collective-permute-start(bf16[4,128,512]{2,1,0:T(8,128)(2,1)S(1)} %get-tuple-element.60.own_ref), channel_id=1, source_target_pairs={{0,3},{1,0},{2,1},{3,2},{4,7},{5,4},{6,5},{7,6},{8,11},{9,8},{10,9... | collective-permute-start | bytes 1572872 | tf_op jit(solution)/shard_map/ppermute | solution.py:400
  24.5 16.8 %collective-permute-start.9 = (bf16[4,128,512]{2,1,0:T(8,128)(2,1)S(1)}, bf16[4,128,512]{2,1,0:T(8,128)(2,1)S(1)}, u32[]{:S(2)}, u32[]{:S(2)}) collective-permute-start(bf16[4,128,512]{2,1,0:T(8,128)(2,1)S(1)} %get-tuple-element.60.own_ref), channel_id=1, source_target_pairs={{0,1},{1,2},{2,3},{3,0},{4,5},{5,6},{6,7},{7,4},{8,9},{9,10},{10,1... | collective-permute-start | bytes 1572872 | tf_op jit(solution)/shard_map/ppermute | solution.py:400
  41.4 20.3 %collective-permute-start.7 = (bf16[512,512]{1,0:T(8,128)(2,1)S(1)}, bf16[512,512]{1,0:T(8,128)(2,1)S(1)}, u32[]{:S(2)}, u32[]{:S(2)}) collective-permute-start(bf16[512,512]{1,0:T(8,128)(2,1)S(1)} %get-tuple-element.58.refs_3_), channel_id=1, source_target_pairs={{0,4},{4,8},{8,12},{12,16},{16,20},{20,24},{24,28},{28,0},{1,5},{5... | collective-permute-start | bytes 1572872 | tf_op jit(solution)/shard_map/ppermute | solution.py:400
  41.5 20.2 %collective-permute-start.8 = (bf16[512,512]{1,0:T(8,128)(2,1)S(1)}, bf16[512,512]{1,0:T(8,128)(2,1)S(1)}, u32[]{:S(2)}, u32[]{:S(2)}) collective-permute-start(bf16[512,512]{1,0:T(8,128)(2,1)S(1)} %get-tuple-element.59.refs_4_), channel_id=1, source_target_pairs={{0,28},{4,0},{8,4},{12,8},{16,12},{20,16},{24,20},{28,24},{1,29},{... | collective-permute-start | bytes 1572872 | tf_op jit(solution)/shard_map/ppermute | solution.py:400
  44.7 17.0 %collective-permute-start.11 = (bf16[2,128,512]{2,1,0:T(8,128)(2,1)S(1)}, bf16[2,128,512]{2,1,0:T(8,128)(2,1)S(1)}, u32[]{:S(2)}, u32[]{:S(2)}) collective-permute-start(bf16[2,128,512]{2,1,0:T(8,128)(2,1)S(1)} %get-tuple-element.61), channel_id=1, source_target_pairs={{0,1},{1,2},{2,3},{3,0},{4,5},{5,6},{6,7},{7,4},{8,9},{9,10},{10,1... | collective-permute-start | bytes 786440 | tf_op jit(solution)/shard_map/ppermute | solution.py:400
  47.9 13.8 %collective-permute-start.12 = (bf16[2,128,512]{2,1,0:T(8,128)(2,1)S(1)}, bf16[2,128,512]{2,1,0:T(8,128)(2,1)S(1)}, u32[]{:S(2)}, u32[]{:S(2)}) collective-permute-start(bf16[2,128,512]{2,1,0:T(8,128)(2,1)S(1)} %get-tuple-element.62), channel_id=1, source_target_pairs={{0,3},{1,0},{2,1},{3,2},{4,7},{5,4},{6,5},{7,6},{8,11},{9,8},{10,9... | collective-permute-start | bytes 786440 | tf_op jit(solution)/shard_map/ppermute | solution.py:400
  62.0 9.9 %collective-permute-start.13 = (bf16[256,512]{1,0:T(8,128)(2,1)S(1)}, bf16[256,512]{1,0:T(8,128)(2,1)S(1)}, u32[]{:S(2)}, u32[]{:S(2)}) collective-permute-start(bf16[256,512]{1,0:T(8,128)(2,1)S(1)} %get-tuple-element.63), channel_id=1, source_target_pairs={{0,4},{4,8},{8,12},{12,16},{16,20},{20,24},{24,28},{28,0},{1,5},{5... | collective-permute-start | bytes 786440 | tf_op jit(solution)/shard_map/ppermute | solution.py:400
  62.1 9.8 %collective-permute-start.14 = (bf16[256,512]{1,0:T(8,128)(2,1)S(1)}, bf16[256,512]{1,0:T(8,128)(2,1)S(1)}, u32[]{:S(2)}, u32[]{:S(2)}) collective-permute-start(bf16[256,512]{1,0:T(8,128)(2,1)S(1)} %get-tuple-element.64), channel_id=1, source_target_pairs={{0,28},{4,0},{8,4},{12,8},{16,12},{20,16},{24,20},{28,24},{1,29},{... | collective-permute-start | bytes 786440 | tf_op jit(solution)/shard_map/ppermute | solution.py:400
  76.2 8.0 %collective-permute-start.18 = (bf16[528,128]{1,0:T(8,128)(2,1)S(1)}, bf16[528,128]{1,0:T(8,128)(2,1)S(1)}, u32[]{:S(2)}, u32[]{:S(2)}) collective-permute-start(bf16[528,128]{1,0:T(8,128)(2,1)S(1)} %get-tuple-element.77.own_ref), channel_id=1, source_target_pairs={{0,2},{1,3},{2,0},{3,1},{4,6},{5,7},{6,4},{7,5},{8,10},{9,11},{10,... | collective-permute-start | bytes 405512 | tf_op jit(solution)/shard_map/ppermute | solution.py:400
  76.9 9.3 %collective-permute-start.17 = (bf16[528,128]{1,0:T(8,128)(2,1)S(1)}, bf16[528,128]{1,0:T(8,128)(2,1)S(1)}, u32[]{:S(2)}, u32[]{:S(2)}) collective-permute-start(bf16[528,128]{1,0:T(8,128)(2,1)S(1)} %get-tuple-element.77.own_ref), channel_id=1, source_target_pairs={{0,3},{1,0},{2,1},{3,2},{4,7},{5,4},{6,5},{7,6},{8,11},{9,8},{10,9... | collective-permute-start | bytes 405512 | tf_op jit(solution)/shard_map/ppermute | solution.py:400
  78.5 10.4 %collective-permute-start.21 = (bf16[1024,128]{1,0:T(8,128)(2,1)S(1)}, bf16[1024,128]{1,0:T(8,128)(2,1)S(1)}, u32[]{:S(2)}, u32[]{:S(2)}) collective-permute-start(bf16[1024,128]{1,0:T(8,128)(2,1)S(1)} %get-tuple-element.81), channel_id=1, source_target_pairs={{0,1},{1,2},{2,3},{3,0},{4,5},{5,6},{6,7},{7,4},{8,9},{9,10},{10,1... | collective-permute-start | bytes 786440 | tf_op jit(solution)/shard_map/ppermute | solution.py:400
  81.2 10.6 %collective-permute-start.22 = (bf16[1024,128]{1,0:T(8,128)(2,1)S(1)}, bf16[1024,128]{1,0:T(8,128)(2,1)S(1)}, u32[]{:S(2)}, u32[]{:S(2)}) collective-permute-start(bf16[1024,128]{1,0:T(8,128)(2,1)S(1)} %get-tuple-element.82), channel_id=1, source_target_pairs={{0,3},{1,0},{2,1},{3,2},{4,7},{5,4},{6,5},{7,6},{8,11},{9,8},{10,9... | collective-permute-start | bytes 786440 | tf_op jit(solution)/shard_map/ppermute | solution.py:400
  91.9 14.1 %collective-permute-start.23 = (bf16[4,512,128]{2,1,0:T(8,128)(2,1)S(1)}, bf16[4,512,128]{2,1,0:T(8,128)(2,1)S(1)}, u32[]{:S(2)}, u32[]{:S(2)}) collective-permute-start(bf16[4,512,128]{2,1,0:T(8,128)(2,1)S(1)} %get-tuple-element.83), channel_id=1, source_target_pairs={{0,1},{1,2},{2,3},{3,0},{4,5},{5,6},{6,7},{7,4},{8,9},{9,10},{10,1... | collective-permute-start | bytes 1572872 | tf_op jit(solution)/shard_map/ppermute | solution.py:400
  92.8 14.6 %collective-permute-start.24 = (bf16[4,512,128]{2,1,0:T(8,128)(2,1)S(1)}, bf16[4,512,128]{2,1,0:T(8,128)(2,1)S(1)}, u32[]{:S(2)}, u32[]{:S(2)}) collective-permute-start(bf16[4,512,128]{2,1,0:T(8,128)(2,1)S(1)} %get-tuple-element.84), channel_id=1, source_target_pairs={{0,3},{1,0},{2,1},{3,2},{4,7},{5,4},{6,5},{7,6},{8,11},{9,8},{10,9... | collective-permute-start | bytes 1572872 | tf_op jit(solution)/shard_map/ppermute | solution.py:400
  94.3 16.0 %collective-permute-start.27 = (bf16[528,128]{1,0:T(8,128)(2,1)S(1)}, bf16[528,128]{1,0:T(8,128)(2,1)S(1)}, u32[]{:S(2)}, u32[]{:S(2)}) collective-permute-start(bf16[528,128]{1,0:T(8,128)(2,1)S(1)} %shard_map.115.after_ref.own), channel_id=1, source_target_pairs={{0,64},{64,128},{128,192},{192,0},{1,65},{65,129},{129,193},{193,1... | collective-permute-start | bytes 405512 | tf_op jit(solution)/shard_map/ppermute | solution.py:400
  94.9 16.8 %collective-permute-start.26 = (bf16[528,128]{1,0:T(8,128)(2,1)S(1)}, bf16[528,128]{1,0:T(8,128)(2,1)S(1)}, u32[]{:S(2)}, u32[]{:S(2)}) collective-permute-start(bf16[528,128]{1,0:T(8,128)(2,1)S(1)} %shard_map.115.after_ref.own), channel_id=1, source_target_pairs={{0,128},{64,192},{128,0},{192,64},{1,129},{65,193},{129,1},{193,65... | collective-permute-start | bytes 405512 | tf_op jit(solution)/shard_map/ppermute | solution.py:400
  96.8 14.8 %collective-permute-start.25 = (bf16[528,128]{1,0:T(8,128)(2,1)S(1)}, bf16[528,128]{1,0:T(8,128)(2,1)S(1)}, u32[]{:S(2)}, u32[]{:S(2)}) collective-permute-start(bf16[528,128]{1,0:T(8,128)(2,1)S(1)} %shard_map.115.after_ref.own), channel_id=1, source_target_pairs={{0,192},{64,0},{128,64},{192,128},{1,193},{65,1},{129,65},{193,129... | collective-permute-start | bytes 405512 | tf_op jit(solution)/shard_map/ppermute | solution.py:400
  107.6 8.1 %collective-permute-start.28 = (bf16[512,128]{1,0:T(8,128)(2,1)S(1)}, bf16[512,128]{1,0:T(8,128)(2,1)S(1)}, u32[]{:S(2)}, u32[]{:S(2)}) collective-permute-start(bf16[512,128]{1,0:T(8,128)(2,1)S(1)} %get-tuple-element.93), channel_id=1, source_target_pairs={{0,64},{64,128},{128,192},{192,0},{1,65},{65,129},{129,193},{193,1... | collective-permute-start | bytes 393224 | tf_op jit(solution)/shard_map/ppermute | solution.py:400
  108.3 7.4 %collective-permute-start.29 = (bf16[512,128]{1,0:T(8,128)(2,1)S(1)}, bf16[512,128]{1,0:T(8,128)(2,1)S(1)}, u32[]{:S(2)}, u32[]{:S(2)}) collective-permute-start(bf16[512,128]{1,0:T(8,128)(2,1)S(1)} %get-tuple-element.94), channel_id=1, source_target_pairs={{0,128},{64,192},{128,0},{192,64},{1,129},{65,193},{129,1},{193,65... | collective-permute-start | bytes 393224 | tf_op jit(solution)/shard_map/ppermute | solution.py:400
  (15 other events, 202.8 us)

commit v4 on v3

--- a/solution.py
+++ b/solution.py
@@ -49,6 +49,7 @@
 
 
 def call(kernel, out, n_in, flops, any_in=0, scratch=(), any_out=False):
+    limit = VMEM_LIMIT if flops > 1 << 22 else VMEM_LIMIT // 2
     vmem = pl.BlockSpec(memory_space=pltpu.VMEM)
     anys = pl.BlockSpec(memory_space=pl.ANY)
     return pl.pallas_call(
@@ -57,7 +58,7 @@
         in_specs=[anys] * any_in + [vmem] * n_in,
         out_specs=tuple(anys if any_out else vmem for _ in out),
         scratch_shapes=scratch,
-        compiler_params=pltpu.CompilerParams(vmem_limit_bytes=VMEM_LIMIT),
+        compiler_params=pltpu.CompilerParams(vmem_limit_bytes=limit),
         cost_estimate=pl.CostEstimate(flops=flops, bytes_accessed=4 << 20, transcendentals=0),
     )
 
@@ -326,7 +327,7 @@
         send_ref[span(h)] = dot(q_ref[:, span(h)], grad, TN).astype(BF)
         return sums
 
-    sums = lax.fori_loop(0, HEADS, step, jnp.zeros((16, HEAD_DIM), F32), unroll=2)
+    sums = lax.fori_loop(0, HEADS, step, jnp.zeros((16, HEAD_DIM), F32), unroll=4)
     send_ref[base:] = sums.astype(BF)
 
 

time: 117 us -> 117 us (level)
  transfers between devices with their start and end apart: 31 -> 31, of which waited for: 13 -> 13; matrix products, arithmetic and copies ran while one was open for 0% -> 0% of each run, Pallas kernels for 15% -> 14%
where the time goes in v4:
time: 117 us; the launch traced here: 116 us
  starting transfers between devices  45.3 us (39%)
  blocking collectives  26.5 us (23%)
  waiting for transfers between devices  21.5 us (18%)
  Pallas kernels  19.1 us (16%)
  local copies, waits for them, and re-layouts  3.02 us (3%)
    ppermute x28, starting transfers between devices, shift(): return lax.ppermute(x, axis, pairs)  44.8 us
    ppermute x28, waiting for transfers between devices, shift(): return lax.ppermute(x, axis, pairs)  19.4 us
    all_to_all x1, blocking collectives, body(): states = lax.all_to_all(state, BLOCKS, 0, 0, tiled=True)  14.3 us
    all_to_all x1, blocking collectives, body(): prior = lax.all_to_all(priors, BLOCKS, 0, 0, tiled=True).reshape(STATE)  12.2 us
    pallas_call x1, Pallas kernels, body(): call(early_kernel, [(SQUARE, F32), wide, ((2, WIDTH, WIDTH), BF)], 3, 1 <...  5.63 us
    pallas_call x1, Pallas kernels, body(): call(post_kernel, [(SQUARE, BF), (SQUARE, F32), (SQUARE, F32), TOKEN], 5,...  4.37 us
    unnamed x16, local copies, waits for them, and re-layouts  3.02 us
  transfers between devices with their start and end apart: 31, of which 13 were waited for; matrix products, arithmetic and copies ran while one was open for 0% of the time, Pallas kernels for 14%

profile of v4, /device:TPU:6, one launch (start us, length us, event | category | flops | bytes accessed | tf_op | source)
XLA Modules:
  0.0 116.3 jit_solution(8937330538123031057)
XLA Ops:
  0.6 2.0 %collective-permute-start = (bf16[512,512]{1,0:T(8,128)(2,1)}, bf16[512,512]{1,0:T(8,128)(2,1)S(1)}, u32[]{:S(2)}, u32[]{:S(2)}) collective-permute-start(bf16[512,512]{1,0:T(8,128)(2,1)} %refs_0_.1), channel_id=1, source_target_pairs={{0,4},{4,8},{8,12},{12,16},{16,20},{20,24},{24,28},{28,0},{1,5},{5... | collective-permute-start | bytes 1572872 | tf_op jit(solution)/shard_map/ppermute | solution.py:401
  2.6 4.0 %collective-permute-start.1 = (bf16[512,512]{1,0:T(8,128)(2,1)}, bf16[512,512]{1,0:T(8,128)(2,1)S(1)}, u32[]{:S(2)}, u32[]{:S(2)}) collective-permute-start(bf16[512,512]{1,0:T(8,128)(2,1)} %refs_0_.1), channel_id=1, source_target_pairs={{0,28},{4,0},{8,4},{12,8},{16,12},{20,16},{24,20},{28,24},{1,29},{... | collective-permute-start | bytes 1572872 | tf_op jit(solution)/shard_map/ppermute | solution.py:401
  6.7 3.2 %collective-permute-start.3 = (bf16[128,512]{1,0:T(8,128)(2,1)}, bf16[128,512]{1,0:T(8,128)(2,1)S(1)}, u32[]{:S(2)}, u32[]{:S(2)}) collective-permute-start(bf16[128,512]{1,0:T(8,128)(2,1)} %own_ref.1), channel_id=1, source_target_pairs={{0,128},{64,192},{128,0},{192,64},{1,129},{65,193},{129,1},{193,65... | collective-permute-start | bytes 393224 | tf_op jit(solution)/shard_map/ppermute | solution.py:401
  10.5 2.6 %collective-permute-start.4 = (bf16[128,512]{1,0:T(8,128)(2,1)}, bf16[128,512]{1,0:T(8,128)(2,1)S(1)}, u32[]{:S(2)}, u32[]{:S(2)}) collective-permute-start(bf16[128,512]{1,0:T(8,128)(2,1)} %own_ref.1), channel_id=1, source_target_pairs={{0,192},{64,0},{128,64},{192,128},{1,193},{65,1},{129,65},{193,129... | collective-permute-start | bytes 393224 | tf_op jit(solution)/shard_map/ppermute | solution.py:401
  16.5 2.1 %collective-permute-done.after1_ref.refs_0_ = bf16[512,512]{1,0:T(8,128)(2,1)S(1)} collective-permute-done((bf16[512,512]{1,0:T(8,128)(2,1)}, bf16[512,512]{1,0:T(8,128)(2,1)S(1)}, u32[]{:S(2)}, u32[]{:S(2)}) %collective-permute-start) | collective-permute-done | bytes 524320 | tf_op jit(solution)/shard_map/ppermute | solution.py:401
  20.4 3.2 %collective-permute-start.6 = (bf16[512,512]{1,0:T(8,128)(2,1)S(1)}, bf16[512,512]{1,0:T(8,128)(2,1)S(1)}, u32[]{:S(2)}, u32[]{:S(2)}) collective-permute-start(bf16[512,512]{1,0:T(8,128)(2,1)S(1)} %get-tuple-element.56.refs_2_), channel_id=1, source_target_pairs={{0,28},{4,0},{8,4},{12,8},{16,12},{20,16},{24,20},{28,24},{1,29},{... | collective-permute-start | bytes 1572872 | tf_op jit(solution)/shard_map/ppermute | solution.py:401
  24.5 2.4 %collective-permute-start.9 = (bf16[4,128,512]{2,1,0:T(8,128)(2,1)S(1)}, bf16[4,128,512]{2,1,0:T(8,128)(2,1)S(1)}, u32[]{:S(2)}, u32[]{:S(2)}) collective-permute-start(bf16[4,128,512]{2,1,0:T(8,128)(2,1)S(1)} %get-tuple-element.60.own_ref), channel_id=1, source_target_pairs={{0,1},{1,2},{2,3},{3,0},{4,5},{5,6},{6,7},{7,4},{8,9},{9,10},{10,1... | collective-permute-start | bytes 1572872 | tf_op jit(solution)/shard_map/ppermute | solution.py:401
  26.9 14.3 %all_to_all.10.in_ref = bf16[32,16,128]{2,1,0:T(8,128)(2,1)S(1)} all-to-all(bf16[32,16,128]{2,1,0:T(8,128)(2,1)S(1)} %get-tuple-element.50), channel_id=1, replica_groups=mesh['y'=4,'core'=2,'tp'=8,'dp'=4] {'y','core','dp'}, dimensions={0} | all-to-all | bytes 262144 | tf_op jit(solution)/shard_map/all_to_all | solution.py:413
  41.5 3.2 %collective-permute-start.8 = (bf16[512,512]{1,0:T(8,128)(2,1)S(1)}, bf16[512,512]{1,0:T(8,128)(2,1)S(1)}, u32[]{:S(2)}, u32[]{:S(2)}) collective-permute-start(bf16[512,512]{1,0:T(8,128)(2,1)S(1)} %get-tuple-element.59.refs_4_), channel_id=1, source_target_pairs={{0,28},{4,0},{8,4},{12,8},{16,12},{20,16},{24,20},{28,24},{1,29},{... | collective-permute-start | bytes 1572872 | tf_op jit(solution)/shard_map/ppermute | solution.py:401
  44.7 3.2 %collective-permute-start.11 = (bf16[2,128,512]{2,1,0:T(8,128)(2,1)S(1)}, bf16[2,128,512]{2,1,0:T(8,128)(2,1)S(1)}, u32[]{:S(2)}, u32[]{:S(2)}) collective-permute-start(bf16[2,128,512]{2,1,0:T(8,128)(2,1)S(1)} %get-tuple-element.61), channel_id=1, source_target_pairs={{0,1},{1,2},{2,3},{3,0},{4,5},{5,6},{6,7},{7,4},{8,9},{9,10},{10,1... | collective-permute-start | bytes 786440 | tf_op jit(solution)/shard_map/ppermute | solution.py:401
  47.9 12.2 %all_to_all.11 = bf16[32,16,128]{2,1,0:T(8,128)(2,1)S(1)} all-to-all(bf16[32,16,128]{2,1,0:T(8,128)(2,1)S(1)} %get-tuple-element.51), channel_id=1, replica_groups=mesh['y'=4,'core'=2,'tp'=8,'dp'=4] {'y','core','dp'}, dimensions={0} | all-to-all | bytes 262144 | tf_op jit(solution)/shard_map/all_to_all | solution.py:429
  62.0 3.2 %collective-permute-start.14 = (bf16[256,512]{1,0:T(8,128)(2,1)S(1)}, bf16[256,512]{1,0:T(8,128)(2,1)S(1)}, u32[]{:S(2)}, u32[]{:S(2)}) collective-permute-start(bf16[256,512]{1,0:T(8,128)(2,1)S(1)} %get-tuple-element.64), channel_id=1, source_target_pairs={{0,28},{4,0},{8,4},{12,8},{16,12},{20,16},{24,20},{28,24},{1,29},{... | collective-permute-start | bytes 786440 | tf_op jit(solution)/shard_map/ppermute | solution.py:401
  66.1 5.6 %shard_map.109 = (f32[512,512]{1,0:T(8,128)S(1)}, bf16[8,512,512]{2,1,0:T(8,128)(2,1)S(1)}, bf16[2,512,512]{2,1,0:T(8,128)(2,1)S(1)}) custom-call(bf16[512,512]{1,0:T(8,128)(2,1)S(1)} %copy-done.7, bf16[512,512]{1,0:T(8,128)(2,1)S(1)} %get-tuple-element.55.refs_1_, bf16[512,512]{1,0:T(8,128)(2,1)S(1)} %get-tuple-element.56.refs_2_, ...), custom_call_target="tpu_custom_call" | custom-call | flops 8589934592 | bytes 4194304 | tf_op jit(solution)/shard_map/pallas_call | solution.py:453
  73.7 1.9 %collective-permute-start.19 = (bf16[528,128]{1,0:T(8,128)(2,1)S(1)}, bf16[528,128]{1,0:T(8,128)(2,1)S(1)}, u32[]{:S(2)}, u32[]{:S(2)}) collective-permute-start(bf16[528,128]{1,0:T(8,128)(2,1)S(1)} %get-tuple-element.77.own_ref), channel_id=1, source_target_pairs={{0,1},{1,2},{2,3},{3,0},{4,5},{5,6},{6,7},{7,4},{8,9},{9,10},{10,1... | collective-permute-start | bytes 405512 | tf_op jit(solution)/shard_map/ppermute | solution.py:401
  77.9 2.6 %collective-permute-start.21 = (bf16[1024,128]{1,0:T(8,128)(2,1)S(1)}, bf16[1024,128]{1,0:T(8,128)(2,1)S(1)}, u32[]{:S(2)}, u32[]{:S(2)}) collective-permute-start(bf16[1024,128]{1,0:T(8,128)(2,1)S(1)} %get-tuple-element.81), channel_id=1, source_target_pairs={{0,1},{1,2},{2,3},{3,0},{4,5},{5,6},{6,7},{7,4},{8,9},{9,10},{10,1... | collective-permute-start | bytes 786440 | tf_op jit(solution)/shard_map/ppermute | solution.py:401
  80.6 3.0 %collective-permute-done.18.r2_ref = bf16[528,128]{1,0:T(8,128)(2,1)S(1)} collective-permute-done((bf16[528,128]{1,0:T(8,128)(2,1)S(1)}, bf16[528,128]{1,0:T(8,128)(2,1)S(1)}, u32[]{:S(2)}, u32[]{:S(2)}) %collective-permute-start.18) | collective-permute-done | bytes 135200 | tf_op jit(solution)/shard_map/ppermute | solution.py:401
  83.6 2.1 %collective-permute-done.17.r1_ref = bf16[528,128]{1,0:T(8,128)(2,1)S(1)} collective-permute-done((bf16[528,128]{1,0:T(8,128)(2,1)S(1)}, bf16[528,128]{1,0:T(8,128)(2,1)S(1)}, u32[]{:S(2)}, u32[]{:S(2)}) %collective-permute-start.17) | collective-permute-done | bytes 135200 | tf_op jit(solution)/shard_map/ppermute | solution.py:401
  88.3 2.8 %collective-permute-done.22.high_ref = bf16[1024,128]{1,0:T(8,128)(2,1)S(1)} collective-permute-done((bf16[1024,128]{1,0:T(8,128)(2,1)S(1)}, bf16[1024,128]{1,0:T(8,128)(2,1)S(1)}, u32[]{:S(2)}, u32[]{:S(2)}) %collective-permute-start.22) | collective-permute-done | bytes 262176 | tf_op jit(solution)/shard_map/ppermute | solution.py:401
  94.1 2.0 %collective-permute-start.26 = (bf16[528,128]{1,0:T(8,128)(2,1)S(1)}, bf16[528,128]{1,0:T(8,128)(2,1)S(1)}, u32[]{:S(2)}, u32[]{:S(2)}) collective-permute-start(bf16[528,128]{1,0:T(8,128)(2,1)S(1)} %shard_map.115.after_ref.own), channel_id=1, source_target_pairs={{0,128},{64,192},{128,0},{192,64},{1,129},{65,193},{129,1},{193,65... | collective-permute-start | bytes 405512 | tf_op jit(solution)/shard_map/ppermute | solution.py:401
  97.4 4.4 %shard_map.111 = (bf16[512,512]{1,0:T(8,128)(2,1)}, f32[512,512]{1,0:T(8,128)S(1)}, f32[512,512]{1,0:T(8,128)S(1)}, f32[8,128]{1,0:T(8,128)S(1)}) custom-call(bf16[512,512]{1,0:T(8,128)(2,1)S(1)} %copy-done.4, bf16[512,512]{1,0:T(8,128)(2,1)S(1)} %copy-done.1, bf16[512,512]{1,0:T(8,128)(2,1)S(1)} %copy-done.3, ...), custom_call_target="tpu_custom_call" | custom-call | flops 2147483648 | bytes 4194304 | tf_op jit(solution)/shard_map/pallas_call | solution.py:489
  101.8 3.5 %collective-permute-done.23.a_ref = bf16[4,512,128]{2,1,0:T(8,128)(2,1)S(1)} collective-permute-done((bf16[4,512,128]{2,1,0:T(8,128)(2,1)S(1)}, bf16[4,512,128]{2,1,0:T(8,128)(2,1)S(1)}, u32[]{:S(2)}, u32[]{:S(2)}) %collective-permute-start.23) | collective-permute-done | bytes 524320 | tf_op jit(solution)/shard_map/ppermute | solution.py:401
  107.5 2.0 %collective-permute-start.29 = (bf16[512,128]{1,0:T(8,128)(2,1)S(1)}, bf16[512,128]{1,0:T(8,128)(2,1)S(1)}, u32[]{:S(2)}, u32[]{:S(2)}) collective-permute-start(bf16[512,128]{1,0:T(8,128)(2,1)S(1)} %get-tuple-element.94), channel_id=1, source_target_pairs={{0,128},{64,192},{128,0},{192,64},{1,129},{65,193},{129,1},{193,65... | collective-permute-start | bytes 393224 | tf_op jit(solution)/shard_map/ppermute | solution.py:401
  110.8 1.6 %shard_map.118 = (bf16[512,512]{1,0:T(8,128)(2,1)}, bf16[512,512]{1,0:T(8,128)(2,1)}, f32[4,128]{1,0:T(4,128)}) custom-call(bf16[512,128]{1,0:T(8,128)(2,1)S(1)} %get-tuple-element.85.after_last_ref, bf16[512,512]{1,0:T(8,128)(2,1)S(1)} %copy-done.1, bf16[512,512]{1,0:T(8,128)(2,1)S(1)} %copy-done.3, f32[512,512]{1,0:T(8,128)S(1)} %get-tuple-element.86.kp_ref, ...), custom_call_target="tpu_custom_call" | custom-call | flops 268435456 | bytes 4194304 | tf_op jit(solution)/shard_map/pallas_call | solution.py:505
  112.4 2.5 %collective-permute-done.28.r1_ref = bf16[512,128]{1,0:T(8,128)(2,1)S(1)} collective-permute-done((bf16[512,128]{1,0:T(8,128)(2,1)S(1)}, bf16[512,128]{1,0:T(8,128)(2,1)S(1)}, u32[]{:S(2)}, u32[]{:S(2)}) %collective-permute-start.28) | collective-permute-done | bytes 131104 | tf_op jit(solution)/shard_map/ppermute | solution.py:401
  (75 shorter events, 25.9 us)
Async XLA Ops:
  0.6 18.1 %collective-permute-start = (bf16[512,512]{1,0:T(8,128)(2,1)}, bf16[512,512]{1,0:T(8,128)(2,1)S(1)}, u32[]{:S(2)}, u32[]{:S(2)}) collective-permute-start(bf16[512,512]{1,0:T(8,128)(2,1)} %refs_0_.1), channel_id=1, source_target_pairs={{0,4},{4,8},{8,12},{12,16},{16,20},{20,24},{24,28},{28,0},{1,5},{5... | collective-permute-start | bytes 1572872 | tf_op jit(solution)/shard_map/ppermute | solution.py:401
  2.6 16.1 %collective-permute-start.1 = (bf16[512,512]{1,0:T(8,128)(2,1)}, bf16[512,512]{1,0:T(8,128)(2,1)S(1)}, u32[]{:S(2)}, u32[]{:S(2)}) collective-permute-start(bf16[512,512]{1,0:T(8,128)(2,1)} %refs_0_.1), channel_id=1, source_target_pairs={{0,28},{4,0},{8,4},{12,8},{16,12},{20,16},{24,20},{28,24},{1,29},{... | collective-permute-start | bytes 1572872 | tf_op jit(solution)/shard_map/ppermute | solution.py:401
  6.7 9.4 %collective-permute-start.3 = (bf16[128,512]{1,0:T(8,128)(2,1)}, bf16[128,512]{1,0:T(8,128)(2,1)S(1)}, u32[]{:S(2)}, u32[]{:S(2)}) collective-permute-start(bf16[128,512]{1,0:T(8,128)(2,1)} %own_ref.1), channel_id=1, source_target_pairs={{0,128},{64,192},{128,0},{192,64},{1,129},{65,193},{129,1},{193,65... | collective-permute-start | bytes 393224 | tf_op jit(solution)/shard_map/ppermute | solution.py:401
  20.4 20.9 %collective-permute-start.5 = (bf16[512,512]{1,0:T(8,128)(2,1)S(1)}, bf16[512,512]{1,0:T(8,128)(2,1)S(1)}, u32[]{:S(2)}, u32[]{:S(2)}) collective-permute-start(bf16[512,512]{1,0:T(8,128)(2,1)S(1)} %get-tuple-element.55.refs_1_), channel_id=1, source_target_pairs={{0,4},{4,8},{8,12},{12,16},{16,20},{20,24},{24,28},{28,0},{1,5},{5... | collective-permute-start | bytes 1572872 | tf_op jit(solution)/shard_map/ppermute | solution.py:401
  20.4 20.8 %collective-permute-start.6 = (bf16[512,512]{1,0:T(8,128)(2,1)S(1)}, bf16[512,512]{1,0:T(8,128)(2,1)S(1)}, u32[]{:S(2)}, u32[]{:S(2)}) collective-permute-start(bf16[512,512]{1,0:T(8,128)(2,1)S(1)} %get-tuple-element.56.refs_2_), channel_id=1, source_target_pairs={{0,28},{4,0},{8,4},{12,8},{16,12},{20,16},{24,20},{28,24},{1,29},{... | collective-permute-start | bytes 1572872 | tf_op jit(solution)/shard_map/ppermute | solution.py:401
  23.7 17.6 %collective-permute-start.10 = (bf16[4,128,512]{2,1,0:T(8,128)(2,1)S(1)}, bf16[4,128,512]{2,1,0:T(8,128)(2,1)S(1)}, u32[]{:S(2)}, u32[]{:S(2)}) collective-permute-start(bf16[4,128,512]{2,1,0:T(8,128)(2,1)S(1)} %get-tuple-element.60.own_ref), channel_id=1, source_target_pairs={{0,3},{1,0},{2,1},{3,2},{4,7},{5,4},{6,5},{7,6},{8,11},{9,8},{10,9... | collective-permute-start | bytes 1572872 | tf_op jit(solution)/shard_map/ppermute | solution.py:401
  24.5 16.8 %collective-permute-start.9 = (bf16[4,128,512]{2,1,0:T(8,128)(2,1)S(1)}, bf16[4,128,512]{2,1,0:T(8,128)(2,1)S(1)}, u32[]{:S(2)}, u32[]{:S(2)}) collective-permute-start(bf16[4,128,512]{2,1,0:T(8,128)(2,1)S(1)} %get-tuple-element.60.own_ref), channel_id=1, source_target_pairs={{0,1},{1,2},{2,3},{3,0},{4,5},{5,6},{6,7},{7,4},{8,9},{9,10},{10,1... | collective-permute-start | bytes 1572872 | tf_op jit(solution)/shard_map/ppermute | solution.py:401
  41.4 20.3 %collective-permute-start.7 = (bf16[512,512]{1,0:T(8,128)(2,1)S(1)}, bf16[512,512]{1,0:T(8,128)(2,1)S(1)}, u32[]{:S(2)}, u32[]{:S(2)}) collective-permute-start(bf16[512,512]{1,0:T(8,128)(2,1)S(1)} %get-tuple-element.58.refs_3_), channel_id=1, source_target_pairs={{0,4},{4,8},{8,12},{12,16},{16,20},{20,24},{24,28},{28,0},{1,5},{5... | collective-permute-start | bytes 1572872 | tf_op jit(solution)/shard_map/ppermute | solution.py:401
  41.5 20.2 %collective-permute-start.8 = (bf16[512,512]{1,0:T(8,128)(2,1)S(1)}, bf16[512,512]{1,0:T(8,128)(2,1)S(1)}, u32[]{:S(2)}, u32[]{:S(2)}) collective-permute-start(bf16[512,512]{1,0:T(8,128)(2,1)S(1)} %get-tuple-element.59.refs_4_), channel_id=1, source_target_pairs={{0,28},{4,0},{8,4},{12,8},{16,12},{20,16},{24,20},{28,24},{1,29},{... | collective-permute-start | bytes 1572872 | tf_op jit(solution)/shard_map/ppermute | solution.py:401
  44.7 16.9 %collective-permute-start.11 = (bf16[2,128,512]{2,1,0:T(8,128)(2,1)S(1)}, bf16[2,128,512]{2,1,0:T(8,128)(2,1)S(1)}, u32[]{:S(2)}, u32[]{:S(2)}) collective-permute-start(bf16[2,128,512]{2,1,0:T(8,128)(2,1)S(1)} %get-tuple-element.61), channel_id=1, source_target_pairs={{0,1},{1,2},{2,3},{3,0},{4,5},{5,6},{6,7},{7,4},{8,9},{9,10},{10,1... | collective-permute-start | bytes 786440 | tf_op jit(solution)/shard_map/ppermute | solution.py:401
  47.9 13.8 %collective-permute-start.12 = (bf16[2,128,512]{2,1,0:T(8,128)(2,1)S(1)}, bf16[2,128,512]{2,1,0:T(8,128)(2,1)S(1)}, u32[]{:S(2)}, u32[]{:S(2)}) collective-permute-start(bf16[2,128,512]{2,1,0:T(8,128)(2,1)S(1)} %get-tuple-element.62), channel_id=1, source_target_pairs={{0,3},{1,0},{2,1},{3,2},{4,7},{5,4},{6,5},{7,6},{8,11},{9,8},{10,9... | collective-permute-start | bytes 786440 | tf_op jit(solution)/shard_map/ppermute | solution.py:401
  62.0 9.9 %collective-permute-start.13 = (bf16[256,512]{1,0:T(8,128)(2,1)S(1)}, bf16[256,512]{1,0:T(8,128)(2,1)S(1)}, u32[]{:S(2)}, u32[]{:S(2)}) collective-permute-start(bf16[256,512]{1,0:T(8,128)(2,1)S(1)} %get-tuple-element.63), channel_id=1, source_target_pairs={{0,4},{4,8},{8,12},{12,16},{16,20},{20,24},{24,28},{28,0},{1,5},{5... | collective-permute-start | bytes 786440 | tf_op jit(solution)/shard_map/ppermute | solution.py:401
  62.0 9.8 %collective-permute-start.14 = (bf16[256,512]{1,0:T(8,128)(2,1)S(1)}, bf16[256,512]{1,0:T(8,128)(2,1)S(1)}, u32[]{:S(2)}, u32[]{:S(2)}) collective-permute-start(bf16[256,512]{1,0:T(8,128)(2,1)S(1)} %get-tuple-element.64), channel_id=1, source_target_pairs={{0,28},{4,0},{8,4},{12,8},{16,12},{20,16},{24,20},{28,24},{1,29},{... | collective-permute-start | bytes 786440 | tf_op jit(solution)/shard_map/ppermute | solution.py:401
  75.6 8.0 %collective-permute-start.18 = (bf16[528,128]{1,0:T(8,128)(2,1)S(1)}, bf16[528,128]{1,0:T(8,128)(2,1)S(1)}, u32[]{:S(2)}, u32[]{:S(2)}) collective-permute-start(bf16[528,128]{1,0:T(8,128)(2,1)S(1)} %get-tuple-element.77.own_ref), channel_id=1, source_target_pairs={{0,2},{1,3},{2,0},{3,1},{4,6},{5,7},{6,4},{7,5},{8,10},{9,11},{10,... | collective-permute-start | bytes 405512 | tf_op jit(solution)/shard_map/ppermute | solution.py:401
  76.3 9.3 %collective-permute-start.17 = (bf16[528,128]{1,0:T(8,128)(2,1)S(1)}, bf16[528,128]{1,0:T(8,128)(2,1)S(1)}, u32[]{:S(2)}, u32[]{:S(2)}) collective-permute-start(bf16[528,128]{1,0:T(8,128)(2,1)S(1)} %get-tuple-element.77.own_ref), channel_id=1, source_target_pairs={{0,3},{1,0},{2,1},{3,2},{4,7},{5,4},{6,5},{7,6},{8,11},{9,8},{10,9... | collective-permute-start | bytes 405512 | tf_op jit(solution)/shard_map/ppermute | solution.py:401
  77.9 10.4 %collective-permute-start.21 = (bf16[1024,128]{1,0:T(8,128)(2,1)S(1)}, bf16[1024,128]{1,0:T(8,128)(2,1)S(1)}, u32[]{:S(2)}, u32[]{:S(2)}) collective-permute-start(bf16[1024,128]{1,0:T(8,128)(2,1)S(1)} %get-tuple-element.81), channel_id=1, source_target_pairs={{0,1},{1,2},{2,3},{3,0},{4,5},{5,6},{6,7},{7,4},{8,9},{9,10},{10,1... | collective-permute-start | bytes 786440 | tf_op jit(solution)/shard_map/ppermute | solution.py:401
  80.6 10.6 %collective-permute-start.22 = (bf16[1024,128]{1,0:T(8,128)(2,1)S(1)}, bf16[1024,128]{1,0:T(8,128)(2,1)S(1)}, u32[]{:S(2)}, u32[]{:S(2)}) collective-permute-start(bf16[1024,128]{1,0:T(8,128)(2,1)S(1)} %get-tuple-element.82), channel_id=1, source_target_pairs={{0,3},{1,0},{2,1},{3,2},{4,7},{5,4},{6,5},{7,6},{8,11},{9,8},{10,9... | collective-permute-start | bytes 786440 | tf_op jit(solution)/shard_map/ppermute | solution.py:401
  91.3 13.9 %collective-permute-start.23 = (bf16[4,512,128]{2,1,0:T(8,128)(2,1)S(1)}, bf16[4,512,128]{2,1,0:T(8,128)(2,1)S(1)}, u32[]{:S(2)}, u32[]{:S(2)}) collective-permute-start(bf16[4,512,128]{2,1,0:T(8,128)(2,1)S(1)} %get-tuple-element.83), channel_id=1, source_target_pairs={{0,1},{1,2},{2,3},{3,0},{4,5},{5,6},{6,7},{7,4},{8,9},{9,10},{10,1... | collective-permute-start | bytes 1572872 | tf_op jit(solution)/shard_map/ppermute | solution.py:401
  92.0 14.6 %collective-permute-start.24 = (bf16[4,512,128]{2,1,0:T(8,128)(2,1)S(1)}, bf16[4,512,128]{2,1,0:T(8,128)(2,1)S(1)}, u32[]{:S(2)}, u32[]{:S(2)}) collective-permute-start(bf16[4,512,128]{2,1,0:T(8,128)(2,1)S(1)} %get-tuple-element.84), channel_id=1, source_target_pairs={{0,3},{1,0},{2,1},{3,2},{4,7},{5,4},{6,5},{7,6},{8,11},{9,8},{10,9... | collective-permute-start | bytes 1572872 | tf_op jit(solution)/shard_map/ppermute | solution.py:401
  93.4 16.0 %collective-permute-start.27 = (bf16[528,128]{1,0:T(8,128)(2,1)S(1)}, bf16[528,128]{1,0:T(8,128)(2,1)S(1)}, u32[]{:S(2)}, u32[]{:S(2)}) collective-permute-start(bf16[528,128]{1,0:T(8,128)(2,1)S(1)} %shard_map.115.after_ref.own), channel_id=1, source_target_pairs={{0,64},{64,128},{128,192},{192,0},{1,65},{65,129},{129,193},{193,1... | collective-permute-start | bytes 405512 | tf_op jit(solution)/shard_map/ppermute | solution.py:401
  94.1 16.8 %collective-permute-start.26 = (bf16[528,128]{1,0:T(8,128)(2,1)S(1)}, bf16[528,128]{1,0:T(8,128)(2,1)S(1)}, u32[]{:S(2)}, u32[]{:S(2)}) collective-permute-start(bf16[528,128]{1,0:T(8,128)(2,1)S(1)} %shard_map.115.after_ref.own), channel_id=1, source_target_pairs={{0,128},{64,192},{128,0},{192,64},{1,129},{65,193},{129,1},{193,65... | collective-permute-start | bytes 405512 | tf_op jit(solution)/shard_map/ppermute | solution.py:401
  96.0 14.8 %collective-permute-start.25 = (bf16[528,128]{1,0:T(8,128)(2,1)S(1)}, bf16[528,128]{1,0:T(8,128)(2,1)S(1)}, u32[]{:S(2)}, u32[]{:S(2)}) collective-permute-start(bf16[528,128]{1,0:T(8,128)(2,1)S(1)} %shard_map.115.after_ref.own), channel_id=1, source_target_pairs={{0,192},{64,0},{128,64},{192,128},{1,193},{65,1},{129,65},{193,129... | collective-permute-start | bytes 405512 | tf_op jit(solution)/shard_map/ppermute | solution.py:401
  106.8 8.1 %collective-permute-start.28 = (bf16[512,128]{1,0:T(8,128)(2,1)S(1)}, bf16[512,128]{1,0:T(8,128)(2,1)S(1)}, u32[]{:S(2)}, u32[]{:S(2)}) collective-permute-start(bf16[512,128]{1,0:T(8,128)(2,1)S(1)} %get-tuple-element.93), channel_id=1, source_target_pairs={{0,64},{64,128},{128,192},{192,0},{1,65},{65,129},{129,193},{193,1... | collective-permute-start | bytes 393224 | tf_op jit(solution)/shard_map/ppermute | solution.py:401
  107.5 7.4 %collective-permute-start.29 = (bf16[512,128]{1,0:T(8,128)(2,1)S(1)}, bf16[512,128]{1,0:T(8,128)(2,1)S(1)}, u32[]{:S(2)}, u32[]{:S(2)}) collective-permute-start(bf16[512,128]{1,0:T(8,128)(2,1)S(1)} %get-tuple-element.94), channel_id=1, source_target_pairs={{0,128},{64,192},{128,0},{192,64},{1,129},{65,193},{129,1},{193,65... | collective-permute-start | bytes 393224 | tf_op jit(solution)/shard_map/ppermute | solution.py:401
  (15 other events, 161.8 us)
